TPU v7x, 128 devices: a whole 4x4x4 slice. The times are simulated.
128 devices in a mesh: lon: 8 (over x, y_lo), lat: 16 (over z, y_hi, core).
Axes of the slice: x: 4, y: 4 (y_hi: 2, y_lo: 2; y = y_hi * 2 + y_lo), z: 4, core: 2. Of those that a mesh axis runs over, the one named last changes fastest.
Arguments:
- tokens: bfloat16 [2, 384, 192, 512], P(None, 'lat', 'lon'), may hold values from -6 to 6
- cotangent: bfloat16 [2, 384, 192, 512], P(None, 'lat', 'lon'), may hold values from -6 to 6
- valid: int32 [384, 192], P('lat', 'lon'), may hold values 0 or 1
- w_qkv: bfloat16 [512, 1536], replicated, as said below
- w_out: bfloat16 [512, 512], replicated, may hold values from -0.25 to 0.25
- w_up: bfloat16 [512, 2048], replicated, may hold values from -0.25 to 0.25
- w_down: bfloat16 [2048, 512], replicated, may hold values from -0.125 to 0.125
- gains: float32 [2, 512], replicated, may hold values from 0.1 to 1.9
Outputs:
- outputs: bfloat16 [2, 384, 192, 512], P(None, 'lat', 'lon')
- grad_tokens: bfloat16 [2, 384, 192, 512], P(None, 'lat', 'lon')
- grad_qkv: float32 [512, 1536], replicated
- grad_out: float32 [512, 512], replicated
- grad_up: float32 [512, 2048], replicated
- grad_down: float32 [2048, 512], replicated
- grad_gains: float32 [2, 512], replicated
Inputs may be any that keep to these rules, and one draw needn't show every extreme that they name: `w_qkv`: query, key and value columns in this order, heads of 64 side by side.
All inputs are finite; a program needn't handle non-finite values. No bound on the sum of `valid` on one device may be relied on, other than what follows from the above.
Results may differ from a plain program's by a relative error of at most 0.024.
The roundings to bfloat16 on the way count: a program that leaves them out, or rounds other values in their place, can miss the bound.
Values may be sent and summed in bfloat16 or wider, within the bound.
A program may use at most 192 MiB of HBM per device.

v0:
```python
import jax
import jax.numpy as jnp
from jax import lax
from jax.sharding import PartitionSpec as P

HEAD_SIZE = 64
WLAT = 12
WLON = 6


epsilon = 1e-05


def passed_along(value, axis, steps):
    count = lax.axis_size(axis)
    pairs = [(source, (source + steps) % count) for source in range(count)]
    return lax.ppermute(value, axis, pairs)


def normalize(values, gain_row):
    centre = jnp.mean(values, -1, keepdims=True)
    centred = values - centre
    inv_std = lax.rsqrt(jnp.mean(centred * centred, -1, keepdims=True) + epsilon)
    normed = centred * inv_std
    return (normed, inv_std, normed * gain_row)


def norm_back(grad_value, normed, inv_std, gain_row):
    scaled = grad_value * gain_row
    return inv_std * (
        scaled
        - jnp.mean(scaled, -1, keepdims=True)
        - normed * jnp.mean(scaled * normed, -1, keepdims=True)
    )


def to_windows(field):
    levels, lat_rows, lon_cols, channels = field.shape
    shaped = field.reshape(levels, lat_rows // WLAT, WLAT, lon_cols // WLON, WLON, channels)
    return shaped.transpose(1, 3, 0, 2, 4, 5).reshape(-1, levels * WLAT * WLON, channels)


def from_windows(windows, levels, lat_rows, lon_cols):
    channels = windows.shape[-1]
    shaped = windows.reshape(lat_rows // WLAT, lon_cols // WLON, levels, WLAT, WLON, channels)
    return shaped.transpose(2, 0, 3, 1, 4, 5).reshape(levels, lat_rows, lon_cols, channels)


def window_mask(valid_part, first_row, total_rows, levels):
    lat_rows, lon_cols = valid_part.shape
    row_ids = first_row + jnp.arange(lat_rows, dtype=jnp.int32)
    region = (row_ids >= total_rows - WLAT).astype(jnp.int32) + (
        row_ids >= total_rows - WLAT // 2
    ).astype(jnp.int32)
    region = jnp.broadcast_to(region[None, :, None, None], (levels, lat_rows, lon_cols, 1))
    usable = jnp.broadcast_to(valid_part[None, :, :, None], (levels, lat_rows, lon_cols, 1))
    region = to_windows(region)[..., 0]
    usable = to_windows(usable)[..., 0]
    win_size = region.shape[1]
    itself = (
        jnp.arange(win_size, dtype=jnp.int32)[:, None]
        == jnp.arange(win_size, dtype=jnp.int32)[None, :]
    )
    return (region[:, :, None] == region[:, None, :]) & ((usable[:, None, :] == 1) | itself[None])


def roll_ahead(field):
    half_lat = WLAT // 2
    half_lon = WLON // 2
    rim_rows = passed_along(field[:, :half_lat], "lat", -1)
    field = jnp.concatenate([field[:, half_lat:], rim_rows], axis=1)
    rim_cols = passed_along(field[:, :, :half_lon], "lon", -1)
    return jnp.concatenate([field[:, :, half_lon:], rim_cols], axis=2)


def roll_behind(field):
    half_lat = WLAT // 2
    half_lon = WLON // 2
    rim_rows = passed_along(field[:, -half_lat:], "lat", 1)
    field = jnp.concatenate([rim_rows, field[:, :-half_lat]], axis=1)
    rim_cols = passed_along(field[:, :, -half_lon:], "lon", 1)
    return jnp.concatenate([rim_cols, field[:, :, :-half_lon]], axis=2)


def attend(shifted, allowed, w_qkv, w_out):
    levels, lat_rows, lon_cols, channels = shifted.shape
    head_count = channels // HEAD_SIZE
    windows = to_windows(shifted)
    win_count, win_size = (windows.shape[0], windows.shape[1])
    flat_rows = windows.reshape(win_count * win_size, channels)
    packed = jnp.dot(flat_rows, w_qkv, preferred_element_type=jnp.float32).astype(jnp.bfloat16)
    packed = packed.reshape(win_count, win_size, 3, head_count, HEAD_SIZE)
    query_part = packed[:, :, 0]
    key_part = packed[:, :, 1]
    value_part = packed[:, :, 2]
    scores = jnp.einsum(
        "wqhd,wkhd->whqk", query_part, key_part, preferred_element_type=jnp.float32
    ) * HEAD_SIZE ** (-0.5)
    scores = jnp.where(allowed[:, None], scores, -1e30)
    softmax_out = jax.nn.softmax(scores, axis=-1)
    weights = softmax_out.astype(jnp.bfloat16)
    context = jnp.einsum("whqk,wkhd->wqhd", weights, value_part, preferred_element_type=jnp.float32)
    context = context.astype(jnp.bfloat16).reshape(win_count * win_size, channels)
    result = jnp.dot(context, w_out, preferred_element_type=jnp.float32).astype(jnp.bfloat16)
    saved = (flat_rows, query_part, key_part, value_part, softmax_out, weights, context)
    return (
        from_windows(result.reshape(win_count, win_size, channels), levels, lat_rows, lon_cols),
        saved,
    )


def attend_back(grad_field, saved, w_qkv, w_out):
    flat_rows, query_part, key_part, value_part, softmax_out, weights, context = saved
    levels, lat_rows, lon_cols, channels = grad_field.shape
    win_count, win_size = (query_part.shape[0], query_part.shape[1])
    grad_flat = to_windows(grad_field).reshape(win_count * win_size, channels)
    grad_context = jnp.dot(grad_flat, w_out.T, preferred_element_type=jnp.float32).astype(
        jnp.bfloat16
    )
    grad_context = grad_context.reshape(query_part.shape)
    grad_weights = jnp.einsum(
        "wqhd,wkhd->whqk", grad_context, value_part, preferred_element_type=jnp.float32
    )
    grad_value = jnp.einsum(
        "whqk,wqhd->wkhd", weights, grad_context, preferred_element_type=jnp.float32
    ).astype(jnp.bfloat16)
    inner = jnp.sum(softmax_out * grad_weights, -1, keepdims=True)
    grad_scores = (softmax_out * (grad_weights - inner) * HEAD_SIZE ** (-0.5)).astype(jnp.bfloat16)
    grad_query = jnp.einsum(
        "whqk,wkhd->wqhd", grad_scores, key_part, preferred_element_type=jnp.float32
    ).astype(jnp.bfloat16)
    grad_key = jnp.einsum(
        "whqk,wqhd->wkhd", grad_scores, query_part, preferred_element_type=jnp.float32
    ).astype(jnp.bfloat16)
    grad_packed = jnp.stack([grad_query, grad_key, grad_value], axis=2).reshape(
        win_count * win_size, 3 * channels
    )
    grad_shift = jnp.dot(grad_packed, w_qkv.T, preferred_element_type=jnp.float32).astype(
        jnp.bfloat16
    )
    grad_shift = from_windows(
        grad_shift.reshape(win_count, win_size, channels), levels, lat_rows, lon_cols
    )
    return (grad_shift, (flat_rows, grad_packed), (context, grad_flat))


def feed_forward(mixed, cotangent, gain_row, w_up, w_down):
    channels = mixed.shape[-1]
    mixed_rows = mixed.reshape(-1, channels)
    normed, inv_std, scaled = normalize(mixed_rows, gain_row)
    hidden_in = scaled.astype(jnp.bfloat16)
    raised = jnp.dot(hidden_in, w_up, preferred_element_type=jnp.float32)
    activated = jax.nn.gelu(raised).astype(jnp.bfloat16)
    result = (mixed_rows + jnp.dot(activated, w_down, preferred_element_type=jnp.float32)).astype(
        jnp.bfloat16
    )
    grad_rows = cotangent.reshape(-1, channels)
    grad_act = jnp.dot(grad_rows, w_down.T, preferred_element_type=jnp.float32)
    grad_raised = jax.vjp(jax.nn.gelu, raised)[1](grad_act)[0].astype(jnp.bfloat16)
    grad_in = jnp.dot(grad_raised, w_up.T, preferred_element_type=jnp.float32)
    gain_grad = jnp.sum(grad_in * normed, 0)
    grad_mixed = grad_rows.astype(jnp.float32) + norm_back(grad_in, normed, inv_std, gain_row)
    return (
        result.reshape(mixed.shape),
        grad_mixed.reshape(mixed.shape),
        gain_grad,
        (hidden_in, grad_raised),
        (activated, grad_rows),
    )


def outer_sum(left_part, right_part):
    return lax.dot_general(
        left_part, right_part, (((0,), (0,)), ((), ())), preferred_element_type=jnp.float32
    )


def on_device(tokens, cotangent, valid, w_qkv, w_out, w_up, w_down, gains):
    levels, lat_rows, lon_cols, channels = tokens.shape
    total_rows = lat_rows * lax.axis_size("lat")
    first_row = lax.axis_index("lat") * lat_rows
    all_tokens = levels * lat_rows * lon_cols * lax.axis_size("lat") * lax.axis_size("lon")
    grad_scale = all_tokens ** (-0.5)
    tokens_wide = tokens.astype(jnp.float32)
    normed1, inv_std1, scaled1 = normalize(tokens_wide, gains[0])
    lowered = scaled1.astype(jnp.bfloat16)
    shifted = roll_ahead(lowered)
    allowed = window_mask(valid, first_row, total_rows, levels)
    attended, saved = attend(shifted, allowed, w_qkv, w_out)
    mixed = tokens_wide + roll_behind(attended).astype(jnp.float32)
    outputs, grad_mixed, gain_two, up_pair, down_pair = feed_forward(
        mixed, cotangent, gains[1], w_up, w_down
    )
    grad_attended = roll_ahead(grad_mixed.astype(jnp.bfloat16))
    grad_shifted, qkv_pair, out_pair = attend_back(grad_attended, saved, w_qkv, w_out)
    grad_lowered = roll_behind(grad_shifted).astype(jnp.float32)
    gain_one = jnp.sum(grad_lowered * normed1, axis=(0, 1, 2))
    grad_tokens = (grad_mixed + norm_back(grad_lowered, normed1, inv_std1, gains[0])).astype(
        jnp.bfloat16
    )
    gain_part = jnp.stack([gain_one, gain_two])
    qkv_sum = outer_sum(*qkv_pair)
    out_sum = outer_sum(*out_pair)
    up_sum = outer_sum(*up_pair)
    down_sum = outer_sum(*down_pair)
    summed = lax.psum((qkv_sum, out_sum, up_sum, down_sum, gain_part), ("lon", "lat"))
    return (
        outputs,
        grad_tokens,
        summed[0] * grad_scale,
        summed[1] * grad_scale,
        summed[2] * grad_scale,
        summed[3] * grad_scale,
        summed[4] * grad_scale,
    )


def solution(mesh):
    in_specs = (
        P(None, "lat", "lon", None),
        P(None, "lat", "lon", None),
        P("lat", "lon"),
        P(),
        P(),
        P(),
        P(),
        P(),
    )
    out_specs = (P(None, "lat", "lon", None), P(None, "lat", "lon", None), P(), P(), P(), P(), P())
    return jax.shard_map(
        on_device, mesh=mesh, in_specs=in_specs, out_specs=out_specs, check_vma=False
    )
```

profile of v0, /device:TPU:1, one launch (start us, length us, event | category | flops | bytes accessed | tf_op | source)
XLA Modules:
  0.0 453.2 jit_solution(4707591134660180595)
XLA Ops:
  38.3 5.6 %convolution_convert_fusion = bf16[1152,1536]{1,0:T(8,128)(2,1)} fusion(bf16[1152,512]{1,0:T(8,128)(2,1)} %reshape_reshape.12, bf16[512,1536]{1,0:T(8,128)(2,1)} %param.11), kind=kOutput, calls=%fused_computation.17 | convolution fusion | flops 1813708800 | bytes 6291456 | tf_op jit(solution)/shard_map/dot_general | solution.py:91
  43.9 9.5 %reshape.175 = bf16[8,144,3,8,64]{4,3,2,1,0:T(8,128)(2,1)} reshape(bf16[1152,1536]{1,0:T(8,128)(2,1)} %convolution_convert_fusion) | data formatting | bytes 7077888 | tf_op jit(solution)/shard_map/reshape | solution.py:92
  53.4 6.2 %fusion.76 = (bf16[8,144,1,8,64]{4,3,2,1,0:T(8,128)(2,1)}, bf16[8,144,1,8,64]{4,3,2,1,0:T(8,128)(2,1)}, bf16[8,144,1,8,64]{4,3,2,1,0:T(8,128)(2,1)}) fusion(bf16[8,144,3,8,64]{4,3,2,1,0:T(8,128)(2,1)} %reshape.175), kind=kLoop, calls=%fused_computation.119 | loop fusion | bytes 7077888 | tf_op jit(solution)/shard_map/slice | solution.py:93
  76.8 5.1 %fusion.78 = (f32[8,8,144]{2,1,0:T(8,128)S(1)}, f32[8,8,144,144]{2,3,1,0:T(8,128)}) fusion(f32[8,8,144,144]{2,3,1,0:T(8,128)S(1)} %fusion.41, pred[8,144,144]{1,2,0:T(8,128)(4,1)S(1)} %copy-done.21), kind=kOutput, calls=%fused_computation.121 | output fusion | flops 7962767 | bytes 10819584 | tf_op jit(solution)/shard_map/sub | solution.py:100
  81.8 5.2 %convert_bitcast_fusion.3 = bf16[8,144,8,64]{1,3,2,0:T(8,128)(2,1)S(1)} fusion(bf16[8,144,1,8,64]{1,4,3,0,2:T(8,128)(2,1)} %copy.111, f32[8,8,144,144]{2,3,1,0:T(8,128)} %get-tuple-element.47, f32[8,8,144]{2,1,0:T(8,128)S(1)} %get-tuple-element.46), kind=kOutput, calls=%fused_computation.73 | convolution fusion | flops 173113344 | bytes 7704576 | tf_op jit(solution)/shard_map/whqk,wkhd->wqhd/dot_general | solution.py:102
  89.6 4.8 %reshape.165 = bf16[1152,512]{0,1:T(8,128)(2,1)} reshape(bf16[8,144,8,64]{1,0,3,2:T(8,128)(2,1)} %copy.86) | data formatting | bytes 2359296 | tf_op jit(solution)/shard_map/reshape | solution.py:103
  109.5 6.2 %collective-permute-done.3 = bf16[2,24,3,512]{3,0,2,1:T(2,128)(2,1)S(1)} collective-permute-done((bf16[2,24,3,512]{3,0,2,1:T(2,128)(2,1)S(1)}, bf16[2,24,3,512]{3,0,2,1:T(2,128)(2,1)S(1)}, u32[]{:S(2)}, u32[]{:S(2)}) %collective-permute-start.3) | collective-permute-done | bytes 147488 | tf_op jit(solution)/shard_map/ppermute | solution.py:17
  134.3 5.2 %fusion.73 = f32[2048,512]{1,0:T(8,128)} fusion(bf16[1152,512]{1,0:T(8,128)(2,1)S(1)} %bitcast.113, f32[1152,2048]{1,0:T(8,128)S(1)} %fusion.79), kind=kOutput, calls=%fused_computation.117 | convolution fusion | flops 2437152768 | bytes 14811136 | tf_op jit(solution)/shard_map/dot_general | solution.py:173
  139.6 8.3 %fusion.8 = bf16[1152,2048]{1,0:T(8,128)(2,1)S(1)} fusion(f32[1152,2048]{1,0:T(8,128)S(1)} %fusion.79, bf16[1152,512]{1,0:T(8,128)(2,1)S(1)} %bitcast.114, bf16[2048,512]{1,0:T(8,128)(2,1)S(1)} %copy-done.25), kind=kOutput, calls=%fused_computation.10 | convolution fusion | flops 2463105024 | bytes 17432576 | tf_op jit(solution)/shard_map/dot_general | solution.py:158
  152.9 9.3 %collective-permute-start.4 = (bf16[2,6,24,512]{3,0,2,1:T(2,128)(2,1)S(1)}, bf16[2,6,24,512]{3,0,2,1:T(2,128)(2,1)S(1)}, u32[]{:S(2)}, u32[]{:S(2)}) collective-permute-start(bf16[2,6,24,512]{3,0,2,1:T(2,128)(2,1)S(1)} %copy.125), channel_id=1, source_target_pairs={{0,15},{1,0},{2,1},{3,2},{4,3},{5,4},{6,5},{7,6},{8,7},{9,8},{10,9... | collective-permute-start | bytes 884744 | tf_op jit(solution)/shard_map/ppermute | solution.py:17
  187.4 7.5 %convert_bitcast_fusion = bf16[8,144,1,8,64]{1,4,3,0,2:T(8,128)(2,1)} fusion(bf16[8,144,8,64]{1,3,2,0:T(8,128)(2,1)} %copy.94, f32[8,8,144,144]{2,3,1,0:T(8,128)} %get-tuple-element.47, f32[8,8,144]{2,1,0:T(8,128)S(1)} %get-tuple-element.46), kind=kOutput, calls=%fused_computation.70 | convolution fusion | flops 173113344 | bytes 7704576 | tf_op jit(solution)/shard_map/whqk,wqhd->wkhd/dot_general | solution.py:124
  194.9 5.2 %fusion.45 = f32[8,8,144,144]{2,3,1,0:T(8,128)} fusion(bf16[8,144,8,64]{1,3,2,0:T(8,128)(2,1)S(1)} %copy-done.10, bf16[8,144,1,8,64]{1,4,3,0,2:T(8,128)(2,1)S(1)} %copy-done.9), kind=kOutput, calls=%fused_computation.65 | convolution fusion | flops 169869312 | bytes 7667712 | tf_op jit(solution)/shard_map/wqhd,wkhd->whqk/dot_general | solution.py:121
  200.1 17.1 %convert_bitcast_fusion.2 = bf16[8,144,1,8,64]{1,4,3,0,2:T(8,128)(2,1)} fusion(f32[8,8,144,144]{2,3,1,0:T(8,128)} %fusion.45, bf16[8,144,1,8,64]{1,4,3,0,2:T(8,128)(2,1)} %copy.113, f32[8,8,144,144]{2,3,1,0:T(8,128)} %get-tuple-element.47, f32[8,8,144]{2,1,0:T(8,128)S(1)} %get-tuple-element.46), kind=kOutput, calls=%fused_computation.72 | convolution fusion | flops 179758224 | bytes 13012992 | tf_op jit(solution)/shard_map/whqk,wkhd->wqhd/dot_general | solution.py:129
  217.3 16.5 %convert_bitcast_fusion.1 = bf16[8,144,1,8,64]{1,4,3,0,2:T(8,128)(2,1)} fusion(f32[8,8,144,144]{2,3,1,0:T(8,128)} %fusion.45, bf16[8,144,1,8,64]{1,4,3,0,2:T(8,128)(2,1)S(1)} %copy-done.8, f32[8,8,144,144]{2,3,1,0:T(8,128)} %get-tuple-element.47, f32[8,8,144]{2,1,0:T(8,128)S(1)} %get-tuple-element.46), kind=kOutput, calls=%fused_computation.71 | convolution fusion | flops 179758224 | bytes 13012992 | tf_op jit(solution)/shard_map/whqk,wqhd->wkhd/dot_general | solution.py:132
  238.0 7.2 %copy.99 = bf16[8,144,3,8,64]{1,0,4,3,2:T(8,128)(2,1)} copy(bf16[8,144,3,8,64]{1,4,3,0,2:T(8,128)(2,1)S(1)} %pad_maximum_fusion) | data formatting | bytes 7077888 | tf_op jit(solution)/shard_map/stack | solution.py:135
  245.3 10.4 %reshape.173 = bf16[1152,1536]{0,1:T(8,128)(2,1)} reshape(bf16[8,144,3,8,64]{1,0,4,3,2:T(8,128)(2,1)} %copy.99) | data formatting | bytes 7077888 | tf_op jit(solution)/shard_map/reshape | solution.py:135
  255.7 5.9 %fusion.80 = f32[512,1536]{1,0:T(8,128)} fusion(bf16[1152,512]{1,0:T(8,128)(2,1)S(1)} %copy-done.18, bf16[1152,1536]{0,1:T(8,128)(2,1)} %reshape.173), kind=kOutput, calls=%fused_computation.123 | convolution fusion | flops 1811939328 | bytes 7864320 | tf_op jit(solution)/shard_map/dot_general | solution.py:173
  263.0 5.1 %convolution_convert_fusion.1 = bf16[1152,512]{1,0:T(8,128)(2,1)} fusion(bf16[1152,1536]{0,1:T(8,128)(2,1)} %reshape.173, bf16[512,1536]{1,0:T(8,128)(2,1)S(1)} %copy-done.27), kind=kOutput, calls=%fused_computation.30 | convolution fusion | flops 1812529152 | bytes 6291456 | tf_op jit(solution)/shard_map/dot_general | solution.py:138
  273.2 5.5 %collective-permute-done.6 = bf16[2,6,24,512]{3,0,2,1:T(2,128)(2,1)S(1)} collective-permute-done((bf16[2,6,24,512]{3,0,2,1:T(2,128)(2,1)S(1)}, bf16[2,6,24,512]{3,0,2,1:T(2,128)(2,1)S(1)}, u32[]{:S(2)}, u32[]{:S(2)}) %collective-permute-start.6) | collective-permute-done | bytes 294944 | tf_op jit(solution)/shard_map/ppermute | solution.py:17
  279.1 8.4 %fusion.22 = bf16[1152,512]{1,0:T(8,128)(2,1)} fusion(f32[1152,512]{1,0:T(8,128)S(1)} %bitcast.101, bf16[2048,512]{1,0:T(8,128)(2,1)S(1)} %copy-done.26, f32[1152,2048]{1,0:T(8,128)} %copy-done.29), kind=kOutput, calls=%fused_computation.31 | convolution fusion | flops 2438332416 | bytes 15073280 | tf_op jit(solution)/shard_map/dot_general | solution.py:154
  287.6 8.2 %fusion.33 = (f32[512]{0:T(512)S(1)}, f32[2,24,24]{0,2,1:T(8,128)S(1)}, f32[2,24,24]{0,2,1:T(8,128)S(1)}, bf16[2,24,24,512]{3,0,2,1:T(2,128)(2,1)S(1)}) fusion(f32[2,24,24]{0,2,1:T(8,128)S(1)} %copy-done.14, f32[2,24,24]{0,2,1:T(8,128)S(1)} %copy-done.12, bf16[2,24,24,512]{3,2,1,0:T(8,128)(2,1)S(1)} %copy-done.2, f32[512]{0:T(512)S(1)} %bitcast.116, ...), kind=kLoop, calls=%fused_computation.46 | loop fusion | flops 7075072 | bytes 3708928 | tf_op jit(solution)/shard_map/reduce_sum | solution.py:197
  295.8 5.0 %fusion.39 = bf16[2,24,24,512]{3,0,2,1:T(2,128)(2,1)S(1)} fusion(bf16[2,24,24,512]{3,0,2,1:T(2,128)(2,1)S(1)} %get-tuple-element.38, f32[2,24,24,512]{3,2,1,0:T(8,128)S(1)} %bitcast.104, f32[2,24,24]{0,2,1:T(8,128)S(1)} %broadcast_multiply_fusion.4, f32[2,24,24]{0,2,1:T(8,128)S(1)} %broadcast_multiply_fusion.5, f32[512]{0:T(512)S(1)} %bitcast.117, ...), kind=kLoop, calls=%fused_computation.59 | loop fusion | flops 6488064 | bytes 5918720 | tf_op jit(solution)/shard_map/convert_element_type | solution.py:198
  302.1 74.2 %psum.39 = f32[2,512]{1,0:T(2,128)S(1)} all-reduce(f32[2,512]{1,0:T(2,128)S(1)} %pad_maximum_fusion.9), channel_id=1, replica_groups=mesh['lon'=8,'lat'=16] {'lon','lat'}, use_global_device_ids=true, to_apply=%region_17.18 | all-reduce | flops 1024 | bytes 8192 | tf_op jit(solution)/shard_map/psum | solution.py:206
  376.8 58.0 %all-reduce.3.cloned.1.call-done = (f32[512,1536]{1,0:T(8,128)}, f32[512,512]{1,0:T(8,128)}, f32[512,2048]{1,0:T(8,128)}, f32[2048,512]{1,0:T(8,128)}) async-done(((f32[512,1536]{1,0:T(8,128)}, f32[512,512]{1,0:T(8,128)}, f32[512,2048]{1,0:T(8,128)}, f32[2048,512]{1,0:T(8,128)}), (f32[512,1536]{1,0:T(8,128)}, f32[512,512]{1,0:T(8,128)}, f32[512,2048]{1,0:T(8,128)}, ...) | async-done | bytes 12582928 | tf_op jit(solution)/shard_map/psum | solution.py:206
  (152 shorter events, 138.7 us)
Async XLA Ops:
  7.2 124.5 %copy-start = (bf16[512,2048]{1,0:T(8,128)(2,1)S(1)}, bf16[512,2048]{1,0:T(8,128)(2,1)}, u32[]{:S(2)}) copy-start(bf16[512,2048]{1,0:T(8,128)(2,1)} %param.13) | copy-start | bytes 6291460
  7.2 427.6 %all-reduce.3.cloned.1.call-start = ((), (), s32[]{:S(2)}) async-start(), calls=%async_computation | async-start | bytes 25165824 | tf_op jit(solution)/shard_map/psum | solution.py:206
  8.1 7.0 %copy-start.22 = (f32[1,512]{1,0:T(1,128)}, f32[1,512]{1,0:T(1,128)S(1)}, u32[]{:S(2)}) copy-start(f32[1,512]{1,0:T(1,128)S(1)} %get-tuple-element.45) | copy-start | bytes 6148
  13.1 6.0 %copy-start.24 = (s32[24,24]{1,0:T(8,128)S(1)}, s32[24,24]{1,0:T(8,128)}, u32[]{:S(2)}) copy-start(s32[24,24]{1,0:T(8,128)} %param.10) | copy-start | bytes 6916
  16.0 9.0 %collective-permute-start = (bf16[2,6,24,512]{3,0,2,1:T(2,128)(2,1)}, bf16[2,6,24,512]{3,0,2,1:T(2,128)(2,1)}, u32[]{:S(2)}, u32[]{:S(2)}) collective-permute-start(bf16[2,6,24,512]{3,0,2,1:T(2,128)(2,1)} %slice.86), channel_id=1, source_target_pairs={{0,15},{1,0},{2,1},{3,2},{4,3},{5,4},{6,5},{7,6},{8,7},{9,8},{10,9... | collective-permute-start | bytes 884744 | tf_op jit(solution)/shard_map/ppermute | solution.py:17
  26.2 5.9 %collective-permute-start.1 = (bf16[2,24,3,512]{3,0,2,1:T(2,128)(2,1)S(1)}, bf16[2,24,3,512]{3,0,2,1:T(2,128)(2,1)S(1)}, u32[]{:S(2)}, u32[]{:S(2)}) collective-permute-start(bf16[2,24,3,512]{3,0,2,1:T(2,128)(2,1)S(1)} %pad_maximum_fusion.8), channel_id=1, source_target_pairs={{0,112},{16,0},{32,16},{48,32},{64,48},{80,64},{96,80},{112,96},{1... | collective-permute-start | bytes 442376 | tf_op jit(solution)/shard_map/ppermute | solution.py:17
  104.1 4.7 %collective-permute-start.2 = (bf16[2,6,24,512]{3,0,2,1:T(2,128)(2,1)S(1)}, bf16[2,6,24,512]{3,0,2,1:T(2,128)(2,1)S(1)}, u32[]{:S(2)}, u32[]{:S(2)}) collective-permute-start(bf16[2,6,24,512]{3,0,2,1:T(2,128)(2,1)S(1)} %slice.92), channel_id=1, source_target_pairs={{0,1},{1,2},{2,3},{3,4},{4,5},{5,6},{6,7},{7,8},{8,9},{9,10},{10,1... | collective-permute-start | bytes 884744 | tf_op jit(solution)/shard_map/ppermute | solution.py:17
  109.1 6.6 %collective-permute-start.3 = (bf16[2,24,3,512]{3,0,2,1:T(2,128)(2,1)S(1)}, bf16[2,24,3,512]{3,0,2,1:T(2,128)(2,1)S(1)}, u32[]{:S(2)}, u32[]{:S(2)}) collective-permute-start(bf16[2,24,3,512]{3,0,2,1:T(2,128)(2,1)S(1)} %pad_maximum_fusion.7), channel_id=1, source_target_pairs={{0,16},{16,32},{32,48},{48,64},{64,80},{80,96},{96,112},{112,0},{1... | collective-permute-start | bytes 442376 | tf_op jit(solution)/shard_map/ppermute | solution.py:17
  139.6 8.3 %copy-start.3 = (f32[2,24,24,512]{3,2,1,0:T(8,128)S(1)}, f32[2,24,24,512]{3,2,1,0:T(8,128)}, u32[]{:S(2)}) copy-start(f32[2,24,24,512]{3,2,1,0:T(8,128)} %copy.88) | copy-start | bytes 7077892
  152.5 14.1 %copy-start.6 = (f32[1152,512]{1,0:T(8,128)}, f32[1152,512]{1,0:T(8,128)S(1)}, u32[]{:S(2)}) copy-start(f32[1152,512]{1,0:T(8,128)S(1)} %multiply_add_fusion) | copy-start | bytes 7077892
  152.9 14.8 %collective-permute-start.4 = (bf16[2,6,24,512]{3,0,2,1:T(2,128)(2,1)S(1)}, bf16[2,6,24,512]{3,0,2,1:T(2,128)(2,1)S(1)}, u32[]{:S(2)}, u32[]{:S(2)}) collective-permute-start(bf16[2,6,24,512]{3,0,2,1:T(2,128)(2,1)S(1)} %copy.125), channel_id=1, source_target_pairs={{0,15},{1,0},{2,1},{3,2},{4,3},{5,4},{6,5},{7,6},{8,7},{9,8},{10,9... | collective-permute-start | bytes 884744 | tf_op jit(solution)/shard_map/ppermute | solution.py:17
  167.9 5.1 %collective-permute-start.5 = (bf16[2,24,3,512]{3,0,2,1:T(2,128)(2,1)S(1)}, bf16[2,24,3,512]{3,0,2,1:T(2,128)(2,1)S(1)}, u32[]{:S(2)}, u32[]{:S(2)}) collective-permute-start(bf16[2,24,3,512]{3,0,2,1:T(2,128)(2,1)S(1)} %pad_maximum_fusion.6), channel_id=1, source_target_pairs={{0,112},{16,0},{32,16},{48,32},{64,48},{80,64},{96,80},{112,96},{1... | collective-permute-start | bytes 442376 | tf_op jit(solution)/shard_map/ppermute | solution.py:17
  187.4 7.5 %copy-start.9 = (bf16[8,144,1,8,64]{1,4,3,0,2:T(8,128)(2,1)S(1)}, bf16[8,144,1,8,64]{1,4,3,0,2:T(8,128)(2,1)}, u32[]{:S(2)}) copy-start(bf16[8,144,1,8,64]{1,4,3,0,2:T(8,128)(2,1)} %copy.111) | copy-start | bytes 3538948
  187.4 7.5 %copy-start.10 = (bf16[8,144,8,64]{1,3,2,0:T(8,128)(2,1)S(1)}, bf16[8,144,8,64]{1,3,2,0:T(8,128)(2,1)}, u32[]{:S(2)}) copy-start(bf16[8,144,8,64]{1,3,2,0:T(8,128)(2,1)} %copy.94) | copy-start | bytes 3538948
  200.1 17.1 %copy-start.8 = (bf16[8,144,1,8,64]{1,4,3,0,2:T(8,128)(2,1)S(1)}, bf16[8,144,1,8,64]{1,4,3,0,2:T(8,128)(2,1)}, u32[]{:S(2)}) copy-start(bf16[8,144,1,8,64]{1,4,3,0,2:T(8,128)(2,1)} %copy.112) | copy-start | bytes 3538948
  245.3 10.4 %copy-start.18 = (bf16[1152,512]{1,0:T(8,128)(2,1)S(1)}, bf16[1152,512]{1,0:T(8,128)(2,1)}, u32[]{:S(2)}) copy-start(bf16[1152,512]{1,0:T(8,128)(2,1)} %reshape_reshape.12) | copy-start | bytes 3538948
  270.6 8.5 %copy-start.26 = (bf16[2048,512]{1,0:T(8,128)(2,1)S(1)}, bf16[2048,512]{1,0:T(8,128)(2,1)}, u32[]{:S(2)}) copy-start(bf16[2048,512]{1,0:T(8,128)(2,1)} %param.14) | copy-start | bytes 6291460
  272.2 6.8 %copy-start.4 = (f32[2,24,24,512]{3,2,1,0:T(8,128)S(1)}, f32[2,24,24,512]{3,2,1,0:T(8,128)}, u32[]{:S(2)}) copy-start(f32[2,24,24,512]{3,2,1,0:T(8,128)} %copy.88) | copy-start | bytes 7077892
  272.4 6.3 %collective-permute-start.6 = (bf16[2,6,24,512]{3,0,2,1:T(2,128)(2,1)S(1)}, bf16[2,6,24,512]{3,0,2,1:T(2,128)(2,1)S(1)}, u32[]{:S(2)}, u32[]{:S(2)}) collective-permute-start(bf16[2,6,24,512]{3,0,2,1:T(2,128)(2,1)S(1)} %slice.98), channel_id=1, source_target_pairs={{0,1},{1,2},{2,3},{3,4},{4,5},{5,6},{6,7},{7,8},{8,9},{9,10},{10,1... | collective-permute-start | bytes 884744 | tf_op jit(solution)/shard_map/ppermute | solution.py:17
  279.0 8.6 %collective-permute-start.7 = (bf16[2,24,3,512]{3,0,2,1:T(2,128)(2,1)S(1)}, bf16[2,24,3,512]{3,0,2,1:T(2,128)(2,1)S(1)}, u32[]{:S(2)}, u32[]{:S(2)}) collective-permute-start(bf16[2,24,3,512]{3,0,2,1:T(2,128)(2,1)S(1)} %pad_maximum_fusion.5), channel_id=1, source_target_pairs={{0,16},{16,32},{32,48},{48,64},{64,80},{80,96},{96,112},{112,0},{1... | collective-permute-start | bytes 442376 | tf_op jit(solution)/shard_map/ppermute | solution.py:17
  279.1 8.5 %copy-start.12 = (f32[2,24,24]{0,2,1:T(8,128)S(1)}, f32[2,24,24]{0,2,1:T(8,128)}, u32[]{:S(2)}) copy-start(f32[2,24,24]{0,2,1:T(8,128)} %copy-done.11) | copy-start | bytes 13828
  279.1 8.5 %copy-start.14 = (f32[2,24,24]{0,2,1:T(8,128)S(1)}, f32[2,24,24]{0,2,1:T(8,128)}, u32[]{:S(2)}) copy-start(f32[2,24,24]{0,2,1:T(8,128)} %copy-done.13) | copy-start | bytes 13828
  279.1 8.5 %copy-start.23 = (f32[1,512]{1,0:T(1,128)S(1)}, f32[1,512]{1,0:T(1,128)}, u32[]{:S(2)}) copy-start(f32[1,512]{1,0:T(1,128)} %copy-done.22) | copy-start | bytes 6148
  287.5 8.3 %copy-start.7 = (f32[1152,512]{1,0:T(8,128)S(1)}, f32[1152,512]{1,0:T(8,128)}, u32[]{:S(2)}) copy-start(f32[1152,512]{1,0:T(8,128)} %copy-done.6) | copy-start | bytes 7077892
  (15 other events, 56.8 us)
Sparse Core Ops, SparseCore 0:
  261.7 173.0 all-reduce.2
where the time goes:
time: 459 us; the launch traced here: 453 us
  matrix products  112 us (24%)
  local copies, waits for them, and re-layouts  92.9 us (20%)
  waiting for transfers between devices  79 us (17%)
  blocking collectives  74.2 us (16%)
  other arithmetic  62.8 us (14%)
  starting transfers between devices  17.7 us (4%)
  between operations  14.8 us (3%)
    psum x1, blocking collectives, on_device(): lax.psum((qkv_sum, out_sum, up_sum, down_sum, gain_part), ('lon', 'lat'))  74.2 us
    psum x1, waiting for transfers between devices, on_device(): lax.psum((qkv_sum, out_sum, up_sum, down_sum, gain_part), ('lon', 'lat'))  58 us
    ppermute x8, waiting for transfers between devices, passed_along(): return lax.ppermute(value, axis, pairs)  21 us
    dot_general x4, matrix products, outer_sum(): lax.dot_general(left_part, right_part, (((0,), (0,)), ((), ())), preferre...  19.1 us
    unnamed x66, local copies, waits for them, and re-layouts  18.5 us
    ppermute x8, starting transfers between devices, passed_along(): return lax.ppermute(value, axis, pairs)  17.7 us
    dot_general x1, matrix products, attend_back(): jnp.einsum('whqk,wkhd->wqhd', grad_scores, key_part, preferred_element_ty...  17.1 us
    dot_general x1, matrix products, attend_back(): jnp.einsum('whqk,wqhd->wkhd', grad_scores, query_part, preferred_element_...  16.5 us
  transfers between devices with their start and end apart: 9, of which 6 were waited for; matrix products, arithmetic and copies ran while one was open for 10% of the time, Pallas kernels for 0%

commit v1 on v0

v1 whole, which is shorter than its diff:
```python
import functools

import jax
import jax.numpy as jnp
import numpy as np
from jax import lax
from jax.experimental import pallas as pl
from jax.experimental.pallas import tpu as pltpu
from jax.sharding import PartitionSpec as P

F32 = jnp.float32
BF16 = jnp.bfloat16
MESH = pl.DeviceIdType.MESH
HEAD = 64
WIN = 144
TOK = 1152
HALF = 576
D = 512
FF = 2048
COLS = 24
BLOCK = 144
PIECE = 48
epsilon = 1e-05
LOW = -1e30
ONE_WAY = 8
VMEM_BYTES = 60 * 1024 * 1024


def gather_maps():
    into = np.zeros((HALF, HALF + 2 * PIECE), np.float32)
    back = np.zeros((HALF, HALF + 2 * PIECE), np.float32)
    rim_in = np.zeros((4 * PIECE, TOK), np.float32)
    rim_back = np.zeros((2 * PIECE, HALF), np.float32)
    for lev in range(2):
        for half in range(2):
            for r in range(6):
                for col in range(COLS):
                    window = (col // 6) * WIN + lev * 72 + half * 36 + r * 6 + col % 6
                    chunk = (lev * 2 + half) * BLOCK + r * COLS
                    if col + 3 < COLS:
                        into[window, chunk + col + 3] = 1
                        back[chunk + col + 3, window] = 1
                    else:
                        rim = half * PIECE + lev * 18 + r * 3 + col + 3 - COLS
                        into[window, HALF + rim] = 1
                        back[chunk + col + 3 - COLS, HALF + rim] = 1
                        rim_back[rim, window] = 1
    for lev in range(2):
        for block in range(4):
            for r in range(6):
                for col in range(3):
                    rim_in[block * PIECE + lev * 18 + r * 3 + col, lev * HALF + block * BLOCK + r * COLS + col] = 1
    return [jnp.asarray(m, BF16) for m in (into, back, rim_in, rim_back)]


def mm(a, b):
    return lax.dot_general(a, b, (((1,), (0,)), ((), ())), preferred_element_type=F32)


def mm_nt(a, b):
    return lax.dot_general(a, b, (((1,), (1,)), ((), ())), preferred_element_type=F32)


def mm_tn(a, b):
    return lax.dot_general(a, b, (((0,), (0,)), ((), ())), preferred_element_type=F32)


def norm_stats(values):
    centred = values - jnp.mean(values, -1, keepdims=True)
    inv_std = lax.rsqrt(jnp.mean(centred * centred, -1, keepdims=True) + epsilon)
    return centred * inv_std, inv_std


def norm_back(grad_value, normed, inv_std, gain_row):
    scaled = grad_value * gain_row
    return inv_std * (
        scaled
        - jnp.mean(scaled, -1, keepdims=True)
        - normed * jnp.mean(scaled * normed, -1, keepdims=True)
    )


def rows_loop(total, step, body):
    def run(i, carry):
        body(pl.ds(pl.multiple_of(i * step, step), step))
        return carry

    lax.fori_loop(0, total // step, run, 0)


def halo_kernel(tok, cot, rim_map, lat_t, lat_c, rim_t, rim_c, pack_t, pack_c, send, recv):
    lon, lat = lax.axis_index("lon"), lax.axis_index("lat")
    n_lon, n_lat = lax.axis_size("lon"), lax.axis_size("lat")
    lon_m, lon_p = lax.rem(lon + n_lon - 1, n_lon), lax.rem(lon + 1, n_lon)
    lat_m, lat_p = lax.rem(lat + n_lat - 1, n_lat), lax.rem(lat + 1, n_lat)
    barrier = pltpu.get_barrier_semaphore()
    for peer in ((lon, lat_m), (lon, lat_p), (lon_m, lat), (lon_p, lat), (lon_m, lat_m), (lon_p, lat_p)):
        pl.semaphore_signal(barrier, inc=1, device_id=peer, device_id_type=MESH)
    pack_t[...] = mm(rim_map[...], tok[...]).astype(BF16)
    pack_c[...] = mm(rim_map[...], cot[...]).astype(BF16)
    pl.semaphore_wait(barrier, 6)
    copies = []

    def push(src, dst, peer):
        k = len(copies)
        copy = pltpu.make_async_remote_copy(
            src_ref=src, dst_ref=dst, send_sem=send.at[k], recv_sem=recv.at[k], device_id=peer, device_id_type=MESH
        )
        copy.start()
        copies.append(copy)

    for pack, rim, lat_rim, src in ((pack_t, rim_t, lat_t, tok), (pack_c, rim_c, lat_c, cot)):
        rest = pl.ds(PIECE, 3 * PIECE)
        push(pack.at[rest], rim.at[rest], (lon_m, lat))
        push(pack.at[pl.ds(0, PIECE)], rim.at[pl.ds(0, PIECE)], (lon_m, lat_m))
        for lev in range(2):
            push(src.at[pl.ds(lev * HALF, BLOCK)], lat_rim.at[pl.ds(lev * BLOCK, BLOCK)], (lon, lat_m))
    for copy in copies:
        copy.wait()


def halo(tok, cot, rim_map):
    vm = pl.BlockSpec(memory_space=pltpu.VMEM)
    rim = jax.ShapeDtypeStruct((4 * PIECE, D), BF16)
    lat_rim = jax.ShapeDtypeStruct((2 * BLOCK, D), BF16)
    return pl.pallas_call(
        halo_kernel,
        out_shape=(lat_rim, lat_rim, rim, rim),
        in_specs=[vm] * 3,
        out_specs=(vm,) * 4,
        scratch_shapes=[
            pltpu.VMEM((4 * PIECE, D), BF16),
            pltpu.VMEM((4 * PIECE, D), BF16),
            pltpu.SemaphoreType.DMA((8,)),
            pltpu.SemaphoreType.DMA((8,)),
        ],
        compiler_params=pltpu.CompilerParams(collective_id=0, has_side_effects=True, vmem_limit_bytes=VMEM_BYTES),
        name="halo_in",
    )(tok, cot, rim_map)


def window_bias(key_bias, split):
    rows = lax.broadcasted_iota(jnp.int32, (WIN, WIN), 0)
    cols = lax.broadcasted_iota(jnp.int32, (WIN, WIN), 1)
    bias = jnp.where(rows == cols, 0.0, jnp.broadcast_to(key_bias, (WIN, WIN)))
    apart = ((rows // 36) % 2) != ((cols // 36) % 2)
    return bias + jnp.where(apart, split, 0.0)


def scores_t(key2, query_m, bias):
    s = mm_nt(key2, query_m) * HEAD ** (-0.5) + bias
    e = jnp.exp(s - jnp.max(s, 0, keepdims=True))
    return e * (1.0 / jnp.sum(e, 0, keepdims=True))


def head_masks():
    lane = lax.broadcasted_iota(jnp.int32, (WIN, 128), 1)
    return [lane < HEAD, lane >= HEAD]


def split_amount(window):
    last = (lax.axis_index("lat") == lax.axis_size("lat") - 1) & (window >= 4)
    return jnp.where(last, LOW, 0.0).astype(F32)


def forward_kernel(
    tok, cot, lat_t, lat_c, rim_t, rim_c, into, key_bias, w_qkv, w_out, w_up, w_down, gains,
    x_ref, packed, lowered, context, out_win, gmix, grads, gain2,
    src, c_ref, mixed, hid, hid_t, c_t, acc_out, acc_in,
):
    gain_a = gains[0:1, :]
    gain_b = gains[1:2, :]
    for full, lat_rim, rim, dst in ((tok, lat_t, rim_t, x_ref), (cot, lat_c, rim_c, c_ref)):
        for wr in range(2):
            for lev in range(2):
                if wr == 0:
                    src[lev * 288:(lev + 1) * 288, :] = full[lev * HALF + 144:lev * HALF + 432, :]
                else:
                    src[lev * 288:lev * 288 + 144, :] = full[lev * HALF + 432:lev * HALF + 576, :]
                    src[lev * 288 + 144:(lev + 1) * 288, :] = lat_rim[lev * BLOCK:(lev + 1) * BLOCK, :]
            if wr == 0:
                src[HALF:, :] = rim[PIECE:3 * PIECE, :]
            else:
                src[HALF:HALF + PIECE, :] = rim[3 * PIECE:, :]
                src[HALF + PIECE:, :] = rim[:PIECE, :]
            for n in range(2):
                cols = slice(n * 256, (n + 1) * 256)
                dst[wr * HALF:(wr + 1) * HALF, cols] = mm(into[...], src[:, cols]).astype(BF16)

    def first_norm(rows):
        normed, _ = norm_stats(x_ref[rows, :].astype(F32))
        lowered[rows, :] = (normed * gain_a).astype(BF16)

    rows_loop(TOK, WIN, first_norm)

    def project(n, carry):
        cols = pl.ds(pl.multiple_of(n * 256, 256), 256)
        packed[:, cols] = mm(lowered[...], w_qkv[:, cols]).astype(BF16)
        return carry

    lax.fori_loop(0, 6, project, 0)
    masks = head_masks()

    def attend(w, carry):
        rows = pl.ds(pl.multiple_of(w * WIN, WIN), WIN)
        bias = window_bias(key_bias[rows, :], split_amount(w))
        for pair in range(4):
            lanes = slice(pair * 128, (pair + 1) * 128)
            query = packed[rows, lanes]
            key = packed[rows, D + pair * 128:D + (pair + 1) * 128]
            value = packed[rows, 2 * D + pair * 128:2 * D + (pair + 1) * 128]
            total = None
            for mask in masks:
                probs = scores_t(key, jnp.where(mask, query, 0), bias)
                part = mm_tn(probs.astype(BF16), jnp.where(mask, value, 0))
                total = part if total is None else total + part
            context[rows, lanes] = total.astype(BF16)
        return carry

    lax.fori_loop(0, 8, attend, 0)

    def second_norm(rows):
        attended = mm(context[rows, :], w_out[...]).astype(BF16)
        m = x_ref[rows, :].astype(F32) + attended.astype(F32)
        mixed[rows, :] = m
        normed, _ = norm_stats(m)
        hid[rows, :] = (normed * gain_b).astype(BF16)

    rows_loop(TOK, 288, second_norm)
    hid_t[...] = hid[...].T
    c_t[...] = c_ref[...].T
    acc_out[...] = jnp.zeros_like(acc_out)
    acc_in[...] = jnp.zeros_like(acc_in)
    wide = 256

    def columns(n, carry):
        cols = pl.ds(pl.multiple_of(n * wide, wide), wide)
        raised = mm(hid[...], w_up[:, cols])
        slope = np.float32(np.sqrt(2 / np.pi))
        square = raised * raised
        t = jnp.tanh(slope * (raised + np.float32(0.044715) * (square * raised)))
        cdf = 0.5 * (1.0 + t)
        activated = (raised * cdf).astype(BF16)
        deriv = cdf + 0.5 * raised * (1.0 - t * t) * (slope * (1.0 + np.float32(3 * 0.044715) * square))
        grad_act = mm_nt(c_ref[...], w_down[cols, :])
        grad_raised = (grad_act * deriv).astype(BF16)
        acc_out[...] += mm(activated, w_down[cols, :])
        acc_in[...] += mm_nt(grad_raised, w_up[:, cols])
        half = pl.ds(pl.multiple_of(lax.rem(n, 2) * wide, wide), wide)
        up_rows = pl.ds(pl.multiple_of((n // 2) * 512, 512), 512)
        grads[up_rows, half] = mm(hid_t[...], grad_raised)
        down_rows = pl.ds(pl.multiple_of(FF + n * wide, wide), wide)
        grads[down_rows, :] = mm(c_t[...], activated).T
        return carry

    lax.fori_loop(0, FF // wide, columns, 0)
    gain2[...] = jnp.zeros_like(gain2)

    def finish(rows):
        m = mixed[rows, :]
        out_win[rows, :] = (m + acc_out[rows, :]).astype(BF16)
        normed, inv_std = norm_stats(m)
        grad_in = acc_in[rows, :]
        gain2[0:1, :] += jnp.sum(grad_in * normed, 0, keepdims=True)
        gmix[rows, :] = c_ref[rows, :].astype(F32) + norm_back(grad_in, normed, inv_std, gain_b)

    rows_loop(TOK, WIN, finish)


def forward(*args):
    vm = pl.BlockSpec(memory_space=pltpu.VMEM)
    shape = jax.ShapeDtypeStruct
    return pl.pallas_call(
        forward_kernel,
        out_shape=(
            shape((TOK, D), BF16),
            shape((TOK, 3 * D), BF16),
            shape((TOK, D), BF16),
            shape((TOK, D), BF16),
            shape((TOK, D), BF16),
            shape((TOK, D), F32),
            shape((2 * FF, D), F32),
            shape((8, D), F32),
        ),
        in_specs=[vm] * len(args),
        out_specs=(vm,) * 8,
        scratch_shapes=[
            pltpu.VMEM((HALF + 2 * PIECE, D), BF16),
            pltpu.VMEM((TOK, D), BF16),
            pltpu.VMEM((TOK, D), F32),
            pltpu.VMEM((TOK, D), BF16),
            pltpu.VMEM((D, TOK), BF16),
            pltpu.VMEM((D, TOK), BF16),
            pltpu.VMEM((TOK, D), F32),
            pltpu.VMEM((TOK, D), F32),
        ],
        compiler_params=pltpu.CompilerParams(vmem_limit_bytes=VMEM_BYTES),
        name="forward",
    )(*args)


def backward_kernel(
    x_ref, packed, lowered, context, out_win, gmix, key_bias, w_qkv, w_out, gains, rim_back,
    grads, gtok_win, gain1, rims,
    g_att, g_ctx, g_pack, low_t, ctx_t,
):
    gain_a = gains[0:1, :]

    def start(rows):
        g_att[rows, :] = gmix[rows, :].astype(BF16)
        g_ctx[rows, :] = mm_nt(g_att[rows, :], w_out[...]).astype(BF16)

    rows_loop(TOK, 288, start)
    masks = head_masks()

    def attend(w, carry):
        rows = pl.ds(pl.multiple_of(w * WIN, WIN), WIN)
        bias = window_bias(key_bias[rows, :], split_amount(w))
        for pair in range(4):
            lanes = slice(pair * 128, (pair + 1) * 128)
            key_lanes = slice(D + pair * 128, D + (pair + 1) * 128)
            value_lanes = slice(2 * D + pair * 128, 2 * D + (pair + 1) * 128)
            query = packed[rows, lanes]
            key = packed[rows, key_lanes]
            value = packed[rows, value_lanes]
            grad = g_ctx[rows, lanes]
            sums = [None, None, None]
            for mask in masks:
                query_m = jnp.where(mask, query, 0)
                grad_m = jnp.where(mask, grad, 0)
                probs = scores_t(key, query_m, bias)
                g_weights = mm_nt(value, grad_m)
                inner = jnp.sum(probs * g_weights, 0, keepdims=True)
                g_scores = (probs * (g_weights - inner) * HEAD ** (-0.5)).astype(BF16)
                parts = (
                    mm_tn(g_scores, jnp.where(mask, key, 0)),
                    mm(g_scores, query_m),
                    mm(probs.astype(BF16), grad_m),
                )
                sums = [b if a is None else a + b for a, b in zip(sums, parts)]
            g_pack[rows, lanes] = sums[0].astype(BF16)
            g_pack[rows, key_lanes] = sums[1].astype(BF16)
            g_pack[rows, value_lanes] = sums[2].astype(BF16)
        return carry

    lax.fori_loop(0, 8, attend, 0)
    low_t[...] = lowered[...].T
    ctx_t[...] = context[...].T

    def weight(n, carry):
        cols = pl.ds(pl.multiple_of(n * 256, 256), 256)
        half = pl.ds(pl.multiple_of(lax.rem(n, 2) * 256, 256), 256)
        grads[pl.ds(pl.multiple_of((n // 2) * 512, 512), 512), half] = mm(low_t[...], g_pack[:, cols])
        return carry

    lax.fori_loop(0, 6, weight, 0)
    for n in range(2):
        cols = slice(n * 256, (n + 1) * 256)
        grads[3 * D:, cols] = mm(ctx_t[...], g_att[:, cols])
    gain1[...] = jnp.zeros_like(gain1)

    def finish(rows):
        g_low = mm_nt(g_pack[rows, :], w_qkv[...]).astype(BF16).astype(F32)
        normed, inv_std = norm_stats(x_ref[rows, :].astype(F32))
        gain1[0:1, :] += jnp.sum(g_low * normed, 0, keepdims=True)
        gtok_win[rows, :] = (gmix[rows, :] + norm_back(g_low, normed, inv_std, gain_a)).astype(BF16)

    rows_loop(TOK, 288, finish)
    for k, win in enumerate((out_win, gtok_win)):
        for wr in range(2):
            at = (k * 2 + wr) * 2 * PIECE
            rims[at:at + 2 * PIECE, :] = mm(rim_back[...], win[wr * HALF:(wr + 1) * HALF, :]).astype(BF16)


def backward(*args):
    vm = pl.BlockSpec(memory_space=pltpu.VMEM)
    shape = jax.ShapeDtypeStruct
    return pl.pallas_call(
        backward_kernel,
        out_shape=(shape((4 * D, D), F32), shape((TOK, D), BF16), shape((8, D), F32), shape((8 * PIECE, D), BF16)),
        in_specs=[vm] * len(args),
        out_specs=(vm,) * 4,
        scratch_shapes=[
            pltpu.VMEM((TOK, D), BF16),
            pltpu.VMEM((TOK, D), BF16),
            pltpu.VMEM((TOK, 3 * D), BF16),
            pltpu.VMEM((D, TOK), BF16),
            pltpu.VMEM((D, TOK), BF16),
        ],
        compiler_params=pltpu.CompilerParams(vmem_limit_bytes=VMEM_BYTES),
        name="backward",
    )(*args)


ORDERS = ((0, 1, 2), (1, 2, 0), (2, 0, 1))
PART = 1024


def position():
    lon, lat = lax.axis_index("lon"), lax.axis_index("lat")
    y = lax.rem(lax.div(lat, 2), 2) * 2 + lax.rem(lon, 2)
    return [lax.div(lon, 2), y, lax.div(lat, 4)], lax.rem(lat, 2)


def device_at(place, core):
    x, y, z = place
    return (x * 2 + lax.rem(y, 2), z * 4 + lax.div(y, 2) * 2 + core)


def sum_kernel(
    g1, g2, gain1, gain2, rims, out_win, gtok_win, back,
    r1, r2, gains_out, lon_rims, lat_blocks,
    own, other, out_send, pair_recv, send1, recv1, sum1, recv2, sum2, recv3, send_blocks,
    gain_slots, load_sem, pair_s, pair_r, rs_s, rs_r, ag_s, ag_r, halo_s, halo_r, gain_s, gain_r,
):
    place, core = position()
    lon, lat = lax.axis_index("lon"), lax.axis_index("lat")
    n_lon, n_lat = lax.axis_size("lon"), lax.axis_size("lat")
    lon_m, lon_p = lax.rem(lon + n_lon - 1, n_lon), lax.rem(lon + 1, n_lon)
    lat_m, lat_p = lax.rem(lat + n_lat - 1, n_lat), lax.rem(lat + 1, n_lat)
    partner = device_at(place, 1 - core)

    def peer(axis, step):
        there = list(place)
        there[axis] = lax.rem(place[axis] + step, 4)
        return device_at(there, core), there[axis]

    barrier = pltpu.get_barrier_semaphore()
    greet = [partner, (lon_m, lat), (lon_p, lat), (lon, lat_m), (lon, lat_p)]
    greet += [peer(axis, step)[0] for axis in range(3) for step in (1, 2, 3)]
    for device in greet:
        pl.semaphore_signal(barrier, inc=1, device_id=device, device_id_type=MESH)

    def part_rows(which, part):
        return pl.ds(pl.multiple_of(which * 2048 + part * PART, PART), PART) if part < 2 else pl.ds(
            pl.multiple_of(which * PART, PART), PART
        )

    def source(part):
        return g1 if part < 2 else g2

    def result(part):
        return r1 if part < 2 else r2

    loads = []
    for part in range(3):
        for k, (which, dst) in enumerate(((1 - core, other), (core, own))):
            copy = pltpu.make_async_copy(source(part).at[part_rows(which, part)], dst.at[part], load_sem.at[part, k])
            copy.start()
            loads.append(copy)

    def remote(src, dst, s, r, device):
        copy = pltpu.make_async_remote_copy(
            src_ref=src, dst_ref=dst, send_sem=s, recv_sem=r, device_id=device, device_id_type=MESH
        )
        copy.start()
        return copy

    pl.semaphore_wait(barrier, len(greet))
    waits = []
    halo1 = remote(rims, lon_rims, halo_s.at[0], halo_r.at[0], (lon_p, lat))
    gain_slots[0, 0, 0:1, :] = gain1[0:1, :]
    gain_slots[0, 0, 1:2, :] = gain2[0:1, :]
    gain_slots[0, 0, 2:8, :] = jnp.zeros((6, D), F32)
    gain_pair = remote(gain_slots.at[0, 0], gain_slots.at[0, 1], gain_s.at[0, 0], gain_r.at[0, 0], partner)

    pairs = []
    for part in range(3):
        loads[2 * part].wait()

        def lower(rows, part=part):
            out_send[part, rows, :] = other[part, rows, :].astype(BF16)

        rows_loop(PART, 128, lower)
        pairs.append(
            remote(out_send.at[part], pair_recv.at[part], pair_s.at[part], pair_r.at[part], partner)
        )

    stage1 = []
    for part in range(3):
        loads[2 * part + 1].wait()
        pairs[part].wait_recv()
        axis = ORDERS[part][0]

        def add(rows, part=part):
            own[part, rows, :] += pair_recv[part, rows, :].astype(F32)

        rows_loop(PART, 128, add)
        for step in (1, 2, 3):
            device, at = peer(axis, step)
            rows = pl.ds(pl.multiple_of(at * 256, 256), 256)
            send1[part, step - 1] = own[part, rows, :].astype(BF16)
            stage1.append(
                remote(send1.at[part, step - 1], recv1.at[part, step - 1],
                       rs_s.at[0, part, step - 1], rs_r.at[0, part, step - 1], device)
            )
    gain_pair.wait()
    gain_total = gain_slots[0, 0] + gain_slots[0, 1]

    def gains_along(level, total):
        axis = level - 1
        mine = place[axis]
        gain_slots[level, mine] = total
        copies = []
        for step in (1, 2, 3):
            device, _ = peer(axis, step)
            copies.append(
                remote(gain_slots.at[level, mine], gain_slots.at[level, mine],
                       gain_s.at[level, step - 1], gain_r.at[level, step - 1], device)
            )
        return copies

    def gains_sum(level, copies):
        for copy in copies:
            copy.wait()
        return (gain_slots[level, 0] + gain_slots[level, 1]) + (gain_slots[level, 2] + gain_slots[level, 3])

    gain_copies = gains_along(1, gain_total)

    halo1.wait()
    for k, win in enumerate((out_win, gtok_win)):
        at = (k * 2 + 1) * 2 * PIECE
        for lev in range(2):
            pick = slice((lev * 2 + 1) * BLOCK, (lev * 2 + 2) * BLOCK)
            send_blocks[(k * 2 + lev) * BLOCK:(k * 2 + lev + 1) * BLOCK, :] = (
                mm(back[pick, :HALF], win[HALF:, :])
                + mm(back[pick, HALF:], lon_rims[at:at + 2 * PIECE, :])
            ).astype(BF16)
    halo2 = remote(send_blocks, lat_blocks, halo_s.at[1], halo_r.at[1], (lon, lat_p))

    stage2 = []
    for part in range(3):
        for k in range(3):
            stage1[part * 3 + k].wait_recv()
        mine = pl.ds(pl.multiple_of(place[ORDERS[part][0]] * 256, 256), 256)
        sum1[part] = (own[part, mine, :] + recv1[part, 0].astype(F32)) + (
            recv1[part, 1].astype(F32) + recv1[part, 2].astype(F32)
        )
        axis = ORDERS[part][1]
        for step in (1, 2, 3):
            device, at = peer(axis, step)
            rows = pl.ds(pl.multiple_of(at * 64, 64), 64)
            stage2.append(
                remote(sum1.at[part, rows], recv2.at[part, step - 1],
                       rs_s.at[1, part, step - 1], rs_r.at[1, part, step - 1], device)
            )
    gain_total = gains_sum(1, gain_copies)
    gain_copies = gains_along(2, gain_total)
    stage3 = []
    for part in range(3):
        for k in range(3):
            stage2[part * 3 + k].wait_recv()
        mine = pl.ds(pl.multiple_of(place[ORDERS[part][1]] * 64, 64), 64)
        sum2[part] = (sum1[part, mine, :] + recv2[part, 0]) + (recv2[part, 1] + recv2[part, 2])
        axis = ORDERS[part][2]
        for step in (1, 2, 3):
            device, at = peer(axis, step)
            rows = pl.ds(pl.multiple_of(at * 16, 16), 16)
            stage3.append(
                remote(sum2.at[part, rows], recv3.at[part, step - 1],
                       rs_s.at[2, part, step - 1], rs_r.at[2, part, step - 1], device)
            )
    gain_total = gains_sum(2, gain_copies)
    gain_copies = gains_along(3, gain_total)
    scale = np.float32(147456 ** (-0.5))

    def spread(level, part, rows):
        sent = []
        axis = ORDERS[part][2 - level]
        for step in (1, 2, 3):
            device, _ = peer(axis, step)
            sent.append(
                remote(result(part).at[rows], result(part).at[rows],
                       ag_s.at[level, part, step - 1], ag_r.at[level, part, step - 1], device)
            )
        return sent

    def at_rows(part, length):
        base = (core * 2048 + part * PART) if part < 2 else core * PART
        first, second, third = (place[axis] for axis in ORDERS[part])
        for amount, value in ((256, first), (64, second), (16, third)):
            if amount >= length:
                base = base + value * amount
        return pl.ds(pl.multiple_of(base, length), length)

    level0 = []
    for part in range(3):
        for k in range(3):
            stage3[part * 3 + k].wait_recv()
        mine = pl.ds(pl.multiple_of(place[ORDERS[part][2]] * 16, 16), 16)
        total = (sum2[part, mine, :] + recv3[part, 0]) + (recv3[part, 1] + recv3[part, 2])
        rows = at_rows(part, 16)
        result(part)[rows, :] = (total * scale).astype(BF16)
        level0.append(spread(0, part, rows))
    gain_total = gains_sum(3, gain_copies)
    gains_out[...] = gain_total * scale
    level1 = []
    for part in range(3):
        for copy in level0[part]:
            copy.wait()
        level1.append(spread(1, part, at_rows(part, 64)))
    level2 = []
    for part in range(3):
        for copy in level1[part]:
            copy.wait()
        level2.append(spread(2, part, at_rows(part, 256)))
    last = []
    for part in range(3):
        for copy in level2[part]:
            copy.wait()
        rows = part_rows(core, part)
        last.append(remote(result(part).at[rows], result(part).at[rows], ag_s.at[3, part, 0], ag_r.at[3, part, 0], partner))
    for copy in pairs + stage1 + stage2 + stage3:
        copy.wait_send()
    halo2.wait()
    for copy in last:
        copy.wait()


def sum_all(*args):
    vm = pl.BlockSpec(memory_space=pltpu.VMEM)
    hbm = pl.BlockSpec(memory_space=pl.ANY)
    shape = jax.ShapeDtypeStruct
    dma = pltpu.SemaphoreType.DMA
    return pl.pallas_call(
        sum_kernel,
        out_shape=(
            shape((2 * FF, D), BF16),
            shape((4 * D, D), BF16),
            shape((8, D), F32),
            shape((8 * PIECE, D), BF16),
            shape((4 * BLOCK, D), BF16),
        ),
        in_specs=[hbm, hbm] + [vm] * (len(args) - 2),
        out_specs=(vm,) * 5,
        scratch_shapes=[
            pltpu.VMEM((3, PART, D), F32),
            pltpu.VMEM((3, PART, D), F32),
            pltpu.VMEM((3, PART, D), BF16),
            pltpu.VMEM((3, PART, D), BF16),
            pltpu.VMEM((3, 3, 256, D), BF16),
            pltpu.VMEM((3, 3, 256, D), BF16),
            pltpu.VMEM((3, 256, D), F32),
            pltpu.VMEM((3, 3, 64, D), F32),
            pltpu.VMEM((3, 64, D), F32),
            pltpu.VMEM((3, 3, 16, D), F32),
            pltpu.VMEM((4 * BLOCK, D), BF16),
            pltpu.VMEM((4, 4, 8, D), F32),
            dma((3, 2)),
            dma((3,)),
            dma((3,)),
            dma((3, 3, 3)),
            dma((3, 3, 3)),
            dma((4, 3, 3)),
            dma((4, 3, 3)),
            dma((2,)),
            dma((2,)),
            dma((4, 3)),
            dma((4, 3)),
        ],
        compiler_params=pltpu.CompilerParams(collective_id=1, has_side_effects=True, vmem_limit_bytes=VMEM_BYTES),
        name="sum_all",
    )(*args)


def finish_kernel(r1, r2, out_win, gtok_win, lon_rims, lat_blocks, back, outputs, g_tok, g_qkv, g_out, g_up, g_down, src):
    for n in range(4):
        g_up[:, n * D:(n + 1) * D] = r1[n * D:(n + 1) * D, :].astype(F32)
    g_down[...] = r1[FF:, :].astype(F32)
    for n in range(3):
        g_qkv[:, n * D:(n + 1) * D] = r2[n * D:(n + 1) * D, :].astype(F32)
    g_out[...] = r2[3 * D:, :].astype(F32)
    for k, (win, full) in enumerate(((out_win, outputs), (gtok_win, g_tok))):
        for wr in range(2):
            at = (k * 2 + wr) * 2 * PIECE
            src[:HALF, :] = win[wr * HALF:(wr + 1) * HALF, :]
            src[HALF:, :] = lon_rims[at:at + 2 * PIECE, :]
            for lev in range(2):
                if wr == 0:
                    pick, length = slice(lev * 288, (lev + 1) * 288), 288
                    to = lev * HALF + 144
                else:
                    pick, length = slice(lev * 288, lev * 288 + 144), 144
                    to = lev * HALF + 432
                full[to:to + length, :] = mm(back[pick, :], src[...]).astype(BF16)
        for lev in range(2):
            full[lev * HALF:lev * HALF + BLOCK, :] = lat_blocks[(k * 2 + lev) * BLOCK:(k * 2 + lev + 1) * BLOCK, :]


def finish_all(*args):
    vm = pl.BlockSpec(memory_space=pltpu.VMEM)
    shape = jax.ShapeDtypeStruct
    return pl.pallas_call(
        finish_kernel,
        out_shape=(
            shape((TOK, D), BF16),
            shape((TOK, D), BF16),
            shape((D, 3 * D), F32),
            shape((D, D), F32),
            shape((D, FF), F32),
            shape((FF, D), F32),
        ),
        in_specs=[vm] * len(args),
        out_specs=(vm,) * 6,
        scratch_shapes=[pltpu.VMEM((HALF + 2 * PIECE, D), BF16)],
        compiler_params=pltpu.CompilerParams(vmem_limit_bytes=VMEM_BYTES),
        name="finish",
    )(*args)


def on_device(tokens, cotangent, valid, w_qkv, w_out, w_up, w_down, gains):
    into, back, rim_in, rim_back = gather_maps()
    tok = tokens.reshape(TOK, D)
    cot = cotangent.reshape(TOK, D)
    usable = jnp.where(valid == 1, 0.0, LOW).astype(F32)
    usable = usable.reshape(2, 12, 4, 6).transpose(0, 2, 1, 3).reshape(8, 1, 72)
    key_bias = jnp.broadcast_to(usable, (8, 2, 72)).reshape(TOK, 1)
    lat_t, lat_c, rim_t, rim_c = halo(tok, cot, rim_in)
    x, packed, lowered, context, out_win, gmix, g1, gain2 = forward(
        tok, cot, lat_t, lat_c, rim_t, rim_c, into, key_bias, w_qkv, w_out, w_up, w_down, gains
    )
    g2, gtok_win, gain1, rims = backward(
        x, packed, lowered, context, out_win, gmix, key_bias, w_qkv, w_out, gains, rim_back
    )
    r1, r2, gain_sums, lon_rims, lat_blocks = sum_all(g1, g2, gain1, gain2, rims, out_win, gtok_win, back)
    outputs, g_tok, g_qkv, g_out, g_up, g_down = finish_all(r1, r2, out_win, gtok_win, lon_rims, lat_blocks, back)
    return (
        outputs.reshape(tokens.shape),
        g_tok.reshape(tokens.shape),
        g_qkv,
        g_out,
        g_up,
        g_down,
        gain_sums[:2],
    )


def solution(mesh):
    field = P(None, "lat", "lon", None)
    in_specs = (field, field, P("lat", "lon"), P(), P(), P(), P(), P())
    out_specs = (field, field, P(), P(), P(), P(), P())
    return jax.shard_map(on_device, mesh=mesh, in_specs=in_specs, out_specs=out_specs, check_vma=False)
```

time: 459 us -> 200 us (0.44); the launches traced: 453 us -> 200 us
  Pallas kernels: 0 us -> 196 us
  matrix products: 112 us -> 0 us
  local copies, waits for them, and re-layouts: 92.9 us -> 2.74 us
  waiting for transfers between devices: 79 us -> 0 us
  blocking collectives: 74.2 us -> 0 us
  other arithmetic: 62.8 us -> 0.71 us
  starting transfers between devices: 17.7 us -> 0 us
  between operations: 14.8 us -> 0.67 us
    pallas_call x0 -> x5, Pallas kernels: none -> 196 us  [the longest x1 77.3 us: sum_all(): pl.pallas_call(sum_kernel, out_shape=(shape((2 * FF, D), BF16), shape((4...]
    dot_general x18 -> x0, matrix products: 112 us -> none  [the longest x4 19.1 us: outer_sum(): lax.dot_general(left_part, right_part, (((0,), (0,)), ((), ())), preferre...]
    psum x1 -> x0, blocking collectives: 74.2 us -> none  [on_device(): lax.psum((qkv_sum, out_sum, up_sum, down_sum, gain_part), ('lon', 'lat'))]
    psum x1 -> x0, waiting for transfers between devices: 58 us -> none  [on_device(): lax.psum((qkv_sum, out_sum, up_sum, down_sum, gain_part), ('lon', 'lat'))]
    reshape x5 -> x2, local copies, waits for them, and re-layouts: 31.7 us -> 1.12 us  [the longest x1 1.04 us: on_device(): key_bias = jnp.broadcast_to(usable, (8, 2, 72)).reshape(TOK, 1)]
    ppermute x8 -> x0, waiting for transfers between devices: 21 us -> none  [passed_along(): return lax.ppermute(value, axis, pairs)]
    reduce_sum x5 -> x0, other arithmetic: 20.1 us -> none  [the longest x1 8.2 us: on_device(): gain_one = jnp.sum(grad_lowered * normed1, axis=(0, 1, 2))]
    unnamed x66 -> x0, local copies, waits for them, and re-layouts: 18.5 us -> none
  transfers between devices with their start and end apart: 9 -> 0, of which waited for: 6 -> 0; matrix products, arithmetic and copies ran while one was open for 10% -> 0% of each run, Pallas kernels for 0% -> 0%
where the time goes in v1:
time: 200 us
  Pallas kernels  196 us (98%)
  local copies, waits for them, and re-layouts  2.74 us (1%)
    pallas_call x1, Pallas kernels, sum_all(): pl.pallas_call(sum_kernel, out_shape=(shape((2 * FF, D), BF16), shape((4...  77.3 us
    pallas_call x1, Pallas kernels, forward(): pl.pallas_call(forward_kernel, out_shape=(shape((TOK, D), BF16), shape((T...  51.4 us
    pallas_call x1, Pallas kernels, backward(): pl.pallas_call(backward_kernel, out_shape=(shape((4 * D, D), F32), shape(...  31.9 us
    pallas_call x1, Pallas kernels, halo(): pl.pallas_call(halo_kernel, out_shape=(lat_rim, lat_rim, rim, rim), in_sp...  24.2 us
    pallas_call x1, Pallas kernels, finish_all(): pl.pallas_call(finish_kernel, out_shape=(shape((TOK, D), BF16), shape((TO...  10.9 us

profile of v1, /device:TPU:1, one launch (start us, length us, event | category | flops | bytes accessed | tf_op | source)
XLA Modules:
  0.0 199.9 jit_solution(9882923570927466943)
XLA Ops:
  0.6 0.7 compare_select_fusion
  1.3 0.1 copy.19
  1.4 0.1 reshape.36
  1.5 0.1 copy.20
  1.6 0.1 broadcast_in_dim.17
  1.7 1.0 reshape.40.key_bias
  2.8 24.2 %halo_in.1 = (bf16[288,512]{1,0:T(8,128)(2,1)}, bf16[288,512]{1,0:T(8,128)(2,1)}, bf16[192,512]{1,0:T(8,128)(2,1)}, bf16[192,512]{1,0:T(8,128)(2,1)}) custom-call(bf16[1152,512]{1,0:T(8,128)(2,1)} %bitcast.7, bf16[1152,512]{1,0:T(8,128)(2,1)} %bitcast.9, bf16[192,1152]{1,0:T(8,128)(2,1)} %constant.16.clone.rim_map), custom_call_target="tpu_custom_call" | custom-call | tf_op jit(solution)/shard_map/halo_in/pallas_call | solution.py:126
  27.0 51.4 %forward.1 = (bf16[1152,512]{1,0:T(8,128)(2,1)}, bf16[1152,1536]{1,0:T(8,128)(2,1)}, bf16[1152,512]{1,0:T(8,128)(2,1)}, bf16[1152,512]{1,0:T(8,128)(2,1)}, bf16[...) custom-call(bf16[1152,512]{1,0:T(8,128)(2,1)} %bitcast.8, ...), custom_call_target="tpu_custom_call" | custom-call | tf_op jit(solution)/shard_map/forward/pallas_call | solution.py:273
  78.4 31.9 %backward.1 = (f32[2048,512]{1,0:T(8,128)}, bf16[1152,512]{1,0:T(8,128)(2,1)}, f32[8,512]{1,0:T(8,128)}, bf16[384,512]{1,0:T(8,128)(2,1)}) custom-call(bf16[1152,512]{1,0:T(8,128)(2,1)} %get-tuple-element.39.x_ref, bf16[1152,1536]{1,0:T(8,128)(2,1)} %get-tuple-element.40.packed, bf16[1152,512]{1,0:T(8,128)(2,1)} %get-tuple-element.41.lowered, ...), custom_call_target="tpu_custom_call" | custom-call | tf_op jit(solution)/shard_map/backward/pallas_call | solution.py:378
  110.3 77.3 %sum_all.1 = (bf16[4096,512]{1,0:T(8,128)(2,1)}, bf16[2048,512]{1,0:T(8,128)(2,1)}, f32[8,512]{1,0:T(8,128)}, bf16[384,512]{1,0:T(8,128)(2,1)}, bf16[576,512]{1,0:T(8,128)(2,1)}) custom-call(f32[4096,512]{1,0:T(8,128)} %get-tuple-element.38.g1, f32[2048,512]{1,0:T(8,128)} %get-tuple-element.45.g2, f32[8,512]{1,0:T(8,128)} %get-tuple-element.46.gain1, ...), custom_call_target="tpu_custom_call" | custom-call | tf_op jit(solution)/shard_map/sum_all/pallas_call | solution.py:625
  187.6 1.3 slice.3
  188.9 10.9 %finish.1 = (bf16[1152,512]{1,0:T(8,128)(2,1)}, bf16[1152,512]{1,0:T(8,128)(2,1)}, f32[512,1536]{1,0:T(8,128)}, f32[512,512]{1,0:T(8,128)}, f32[512,2048]{1,0:T(8,128)}, /*index=5*/f32[2048,512]{1,0:T(8,128)}) custom-call(bf16[4096,512]{1,0:T(8,128)(2,1)} %get-tuple-element.50.r1, bf16[2048,512]{1,0:T(8,128)(2,1)} %get-tuple-element.51.r2, ...), custom_call_target="tpu_custom_call" | custom-call | tf_op jit(solution)/shard_map/finish/pallas_call | solution.py:693
  (1 shorter events, 0.0 us)

commit v2 on v1

v2 whole, which is shorter than its diff:
```python
import jax
import jax.numpy as jnp
import numpy as np
from jax import lax
from jax.experimental import pallas as pl
from jax.experimental.pallas import tpu as pltpu
from jax.sharding import PartitionSpec as P

F32 = jnp.float32
BF16 = jnp.bfloat16
MESH = pl.DeviceIdType.MESH
HEAD = 64
WIN = 144
TOK = 1152
HALF = 576
D = 512
FF = 2048
COLS = 24
BLOCK = 144
PIECE = 48
epsilon = 1e-05
LOW = -1e30
SCALE = np.float32(147456 ** (-0.5))
ORDERS = ((0, 1, 2), (1, 2, 0), (2, 0, 1))
VMEM_BYTES = 63 * 1024 * 1024


def gather_maps():
    into = np.zeros((HALF, HALF + 2 * PIECE), np.float32)
    back = np.zeros((HALF, HALF + 2 * PIECE), np.float32)
    rim_in = np.zeros((4 * PIECE, TOK), np.float32)
    rim_back = np.zeros((2 * PIECE, HALF), np.float32)
    for lev in range(2):
        for half in range(2):
            for r in range(6):
                for col in range(COLS):
                    window = (col // 6) * WIN + lev * 72 + half * 36 + r * 6 + col % 6
                    chunk = (lev * 2 + half) * BLOCK + r * COLS
                    if col + 3 < COLS:
                        into[window, chunk + col + 3] = 1
                        back[chunk + col + 3, window] = 1
                    else:
                        rim = half * PIECE + lev * 18 + r * 3 + col + 3 - COLS
                        into[window, HALF + rim] = 1
                        back[chunk + col + 3 - COLS, HALF + rim] = 1
                        rim_back[rim, window] = 1
    for lev in range(2):
        for block in range(4):
            for r in range(6):
                for col in range(3):
                    rim_in[block * PIECE + lev * 18 + r * 3 + col, lev * HALF + block * BLOCK + r * COLS + col] = 1
    return [jnp.asarray(m, BF16) for m in (into, back, rim_in, rim_back)]


def mm(a, b):
    return lax.dot_general(a, b, (((1,), (0,)), ((), ())), preferred_element_type=F32)


def mm_nt(a, b):
    return lax.dot_general(a, b, (((1,), (1,)), ((), ())), preferred_element_type=F32)


def mm_tn(a, b):
    return lax.dot_general(a, b, (((0,), (0,)), ((), ())), preferred_element_type=F32)


def norm_stats(values):
    centred = values - jnp.mean(values, -1, keepdims=True)
    inv_std = lax.rsqrt(jnp.mean(centred * centred, -1, keepdims=True) + epsilon)
    return centred * inv_std, inv_std


def norm_back(grad_value, normed, inv_std, gain_row):
    scaled = grad_value * gain_row
    return inv_std * (
        scaled
        - jnp.mean(scaled, -1, keepdims=True)
        - normed * jnp.mean(scaled * normed, -1, keepdims=True)
    )


def rows_loop(total, step, body):
    def run(i, carry):
        body(pl.ds(pl.multiple_of(i * step, step), step))
        return carry

    lax.fori_loop(0, total // step, run, 0)


def window_bias(key_bias, split):
    rows = lax.broadcasted_iota(jnp.int32, (WIN, WIN), 0)
    cols = lax.broadcasted_iota(jnp.int32, (WIN, WIN), 1)
    bias = jnp.where(rows == cols, 0.0, jnp.broadcast_to(key_bias, (WIN, WIN)))
    apart = ((rows // 36) % 2) != ((cols // 36) % 2)
    return bias + jnp.where(apart, split, 0.0)


def scores_t(key2, query_m, bias):
    s = mm_nt(key2, query_m) * HEAD ** (-0.5) + bias
    e = jnp.exp(s - jnp.max(s, 0, keepdims=True))
    return e * (1.0 / jnp.sum(e, 0, keepdims=True))


def head_masks():
    lane = lax.broadcasted_iota(jnp.int32, (WIN, 128), 1)
    return [lane < HEAD, lane >= HEAD]


def split_amount(window):
    last = (lax.axis_index("lat") == lax.axis_size("lat") - 1) & (window >= 4)
    return jnp.where(last, LOW, 0.0).astype(F32)


def position():
    lon, lat = lax.axis_index("lon"), lax.axis_index("lat")
    y = lax.rem(lax.div(lat, 2), 2) * 2 + lax.rem(lon, 2)
    return [lax.div(lon, 2), y, lax.div(lat, 4)], lax.rem(lat, 2)


def device_at(place, core):
    x, y, z = place
    return (x * 2 + lax.rem(y, 2), z * 4 + lax.div(y, 2) * 2 + core)


def remote(src, dst, s, r, device):
    return pltpu.make_async_remote_copy(
        src_ref=src, dst_ref=dst, send_sem=s, recv_sem=r, device_id=device, device_id_type=MESH
    )


def loop(first, last, body):
    def run(i, carry):
        body(i)
        return carry

    lax.fori_loop(first, last, run, 0)


class Sum:
    def __init__(self, order, start, size, own, out, recv1, sum1, recv2, sum2, recv3, fin, result, base, sems, fine):
        self.order, self.start, self.size, self.fine = order, start, size, fine
        self.own, self.out, self.recv1, self.sum1, self.recv2, self.sum2, self.recv3, self.fin = (
            own, out, recv1, sum1, recv2, sum2, recv3, fin
        )
        self.result, self.base, self.sems = result, base, sems
        self.place, self.core = position()
        self.lengths = (size // 4, size // 16, size // 64)

    def peer(self, level, step):
        axis = self.order[level]
        there = list(self.place)
        there[axis] = lax.rem(self.place[axis] + step, 4)
        return device_at(there, self.core), there[axis]

    def mine(self, level):
        return self.place[self.order[level]]

    def block(self, at, level, base=0):
        length = self.lengths[level]
        return pl.ds(pl.multiple_of(base + at * length, length), length)

    def down(self, level, step):
        s, r = self.sems.at[0, level, step - 1], self.sems.at[1, level, step - 1]
        device, at = self.peer(level, step)
        if level == 0:
            return remote(self.out.at[self.block(at, 0, self.start)], self.recv1.at[step - 1], s, r, device)
        if level == 1:
            return remote(self.sum1.at[self.block(at, 1)], self.recv2.at[step - 1], s, r, device)
        if self.fine:
            return remote(self.sum2.at[self.block(at, 2)], self.recv3.at[step - 1], s, r, device)
        slot = self.recv3.at[self.mine(2)]
        return remote(slot, slot, s, r, device)

    def result_rows(self, level):
        at = self.base + self.start
        for k in range(level + 1):
            at = at + self.mine(k) * self.lengths[k]
        return pl.ds(pl.multiple_of(at, self.lengths[level]), self.lengths[level])

    def up(self, level, step):
        s, r = self.sems.at[2, level, step - 1], self.sems.at[3, level, step - 1]
        device, _ = self.peer(level, step)
        rows = self.result.at[self.result_rows(level)]
        top = 2 if self.fine else 1
        return remote(self.fin if level == top else rows, rows, s, r, device)

    def hand(self):
        rows = pl.ds(pl.multiple_of(self.base + self.start, self.size), self.size)
        rows = self.result.at[rows]
        return remote(rows, rows, self.sems.at[0, 3, 0], self.sems.at[1, 3, 0], device_at(self.place, 1 - self.core))

    def keep(self):
        top = 2 if self.fine else 1
        return pltpu.make_async_copy(self.fin, self.result.at[self.result_rows(top)], self.sems.at[0, 3, 1])

    def received(self, make, level):
        for step in (1, 2, 3):
            make(level, step).wait_recv()

    def send(self, make, level):
        for step in (1, 2, 3):
            make(level, step).start()

    def begin(self):
        for step in (1, 2, 3):
            _, at = self.peer(0, step)
            rows = self.block(at, 0, self.start)
            self.out[rows, :] = self.own[rows, :].astype(BF16)
        self.send(self.down, 0)

    def second(self):
        self.received(self.down, 0)
        rows = self.block(self.mine(0), 0, self.start)
        self.sum1[...] = (self.own[rows, :] + self.recv1[0].astype(F32)) + (
            self.recv1[1].astype(F32) + self.recv1[2].astype(F32)
        )
        self.send(self.down, 1)

    def third(self):
        self.received(self.down, 1)
        rows = self.block(self.mine(1), 1)
        total = (self.sum1[rows, :] + self.recv2[0]) + (self.recv2[1] + self.recv2[2])
        if self.fine:
            self.sum2[...] = total
        else:
            self.recv3[self.mine(2)] = total
        self.send(self.down, 2)

    def gather(self):
        self.received(self.down, 2)
        if self.fine:
            rows = self.block(self.mine(2), 2)
            total = (self.sum2[rows, :] + self.recv3[0]) + (self.recv3[1] + self.recv3[2])
        else:
            total = (self.recv3[0] + self.recv3[1]) + (self.recv3[2] + self.recv3[3])
        self.fin[...] = (total * SCALE).astype(BF16)
        self.keep().start()
        self.send(self.up, 2 if self.fine else 1)
        self.keep().wait()

    def gather_next(self, level):
        self.received(self.up, level + 1)
        self.send(self.up, level)

    def gather_pair(self):
        self.received(self.up, 0)
        self.hand().start()

    def end(self):
        for level in range(3):
            for step in (1, 2, 3):
                self.down(level, step).wait_send()
                if level < 2 or self.fine:
                    self.up(level, step).wait_send()
        self.hand().wait()


def block_kernel(
    tok, cot, rim_in, into, rim_back, back_last, key_bias, w_qkv_h, w_out_h, w_up_h, w_down_h, gains,
    r1, r2, gains_out, out_win, gtok_win, lon_rims, lat_blocks,
    w_qkv, w_out, w_up, w_down, lat_t, lat_c, rim_t, rim_c, pack_t, pack_c,
    x_ref, c_ref, lowered, context, hid, hid_t, c_t, g_ctx, packed, g_pack, src, mixed, acc_out, acc_in,
    own1, out1, pair1, recv1a, sum1a, recv2a, sum2a, recv3a, fin_a,
    own2, out2, pair2, recv1b, sum1b, recv2b, recv3b, fin_b,
    rims, send_blocks, gain_slots, gain_part,
    load_sem, halo_s, halo_r, back_s, back_r, pair1_s, pair1_r, pair2_s, pair2_r, sums_a, sums_b, gain_s, gain_r,
):
    place, core = position()
    lon, lat = lax.axis_index("lon"), lax.axis_index("lat")
    n_lon, n_lat = lax.axis_size("lon"), lax.axis_size("lat")
    lon_m, lon_p = lax.rem(lon + n_lon - 1, n_lon), lax.rem(lon + 1, n_lon)
    lat_m, lat_p = lax.rem(lat + n_lat - 1, n_lat), lax.rem(lat + 1, n_lat)
    partner = device_at(place, 1 - core)
    gain_a = gains[0:1, :]
    gain_b = gains[1:2, :]
    masks = head_masks()

    def peer(axis, step):
        there = list(place)
        there[axis] = lax.rem(place[axis] + step, 4)
        return device_at(there, core)

    barrier = pltpu.get_barrier_semaphore()
    greet = [(lon, lat_m), (lon, lat_p), (lon_m, lat), (lon_p, lat), (lon_m, lat_m), (lon_p, lat_p), partner]
    greet += [peer(axis, step) for axis in range(3) for step in (1, 2, 3)]
    for device in greet:
        pl.semaphore_signal(barrier, inc=1, device_id=device, device_id_type=MESH)
    loads = [
        pltpu.make_async_copy(a, b, load_sem.at[k])
        for k, (a, b) in enumerate(
            ((tok, context), (cot, out_win), (w_qkv_h, w_qkv), (w_out_h, w_out), (w_up_h, w_up), (w_down_h, w_down))
        )
    ]
    for copy in loads:
        copy.start()
    loads[0].wait()
    pack_t[...] = mm(rim_in[...], context[...]).astype(BF16)
    loads[1].wait()
    pack_c[...] = mm(rim_in[...], out_win[...]).astype(BF16)
    pl.semaphore_wait(barrier, len(greet))

    halos = []
    rest = pl.ds(PIECE, 3 * PIECE)
    corner = pl.ds(0, PIECE)
    for pack, rim, lat_rim, full in ((pack_t, rim_t, lat_t, context), (pack_c, rim_c, lat_c, out_win)):
        wanted = [
            (pack.at[rest], rim.at[rest], (lon_m, lat)),
            (pack.at[corner], rim.at[corner], (lon_m, lat_m)),
        ]
        for lev in range(2):
            wanted.append(
                (full.at[pl.ds(lev * HALF, BLOCK)], lat_rim.at[pl.ds(lev * BLOCK, BLOCK)], (lon, lat_m))
            )
        for a, b, device in wanted:
            k = len(halos)
            halos.append(remote(a, b, halo_s.at[k], halo_r.at[k], device))
            halos[k].start()

    def enter(full, lat_rim, rim, dst, wr):
        for lev in range(2):
            if wr == 0:
                src[lev * 288:(lev + 1) * 288, :] = full[lev * HALF + 144:lev * HALF + 432, :]
            else:
                src[lev * 288:lev * 288 + 144, :] = full[lev * HALF + 432:lev * HALF + 576, :]
                src[lev * 288 + 144:(lev + 1) * 288, :] = lat_rim[lev * BLOCK:(lev + 1) * BLOCK, :]
        if wr == 0:
            src[HALF:, :] = rim[PIECE:3 * PIECE, :]
        else:
            src[HALF:HALF + PIECE, :] = rim[3 * PIECE:, :]
            src[HALF + PIECE:, :] = rim[:PIECE, :]
        for n in range(2):
            cols = slice(n * 256, (n + 1) * 256)
            dst[wr * HALF:(wr + 1) * HALF, cols] = mm(into[...], src[:, cols]).astype(BF16)

    def attend(w):
        rows = pl.ds(pl.multiple_of(w * WIN, WIN), WIN)
        bias = window_bias(key_bias[rows, :], split_amount(w))
        for pair in range(4):
            lanes = slice(pair * 128, (pair + 1) * 128)
            query = packed[rows, lanes]
            key = packed[rows, D + pair * 128:D + (pair + 1) * 128]
            value = packed[rows, 2 * D + pair * 128:2 * D + (pair + 1) * 128]
            total = None
            for mask in masks:
                probs = scores_t(key, jnp.where(mask, query, 0), bias)
                part = mm_tn(probs.astype(BF16), jnp.where(mask, value, 0))
                total = part if total is None else total + part
            hid[rows, lanes] = total.astype(BF16)

    for wr in range(2):
        for copy in (halos[0:1] if wr == 0 else halos[1:4]):
            copy.wait_recv()
        enter(context, lat_t, rim_t, x_ref, wr)
        if wr == 0:
            loads[2].wait()

        def first_norm(i, wr=wr):
            rows = pl.ds(pl.multiple_of(wr * HALF + i * WIN, WIN), WIN)
            normed, _ = norm_stats(x_ref[rows, :].astype(F32))
            lowered[rows, :] = (normed * gain_a).astype(BF16)

        loop(0, 4, first_norm)
        band = slice(wr * HALF, (wr + 1) * HALF)

        def project(n, band=band):
            cols = pl.ds(pl.multiple_of(n * 256, 256), 256)
            packed[band, cols] = mm(lowered[band, :], w_qkv[:, cols]).astype(BF16)

        loop(0, 6, project)
        loop(4 * wr, 4 * wr + 4, attend)
    for copy in halos[4:8]:
        copy.wait_recv()
    for wr in range(2):
        enter(out_win, lat_c, rim_c, c_ref, wr)
    for copy in halos:
        copy.wait_send()
    loads[3].wait()
    context[...] = hid[...]

    def second_norm(rows):
        attended = mm(context[rows, :], w_out[...]).astype(BF16)
        m = x_ref[rows, :].astype(F32) + attended.astype(F32)
        mixed[rows, :] = m
        normed, _ = norm_stats(m)
        hid[rows, :] = (normed * gain_b).astype(BF16)

    rows_loop(TOK, 288, second_norm)
    hid_t[...] = hid[...].T
    c_t[...] = c_ref[...].T
    acc_out[...] = jnp.zeros_like(acc_out)
    acc_in[...] = jnp.zeros_like(acc_in)
    loads[4].wait()
    loads[5].wait()

    sum_a = [
        Sum(ORDERS[p], p * 1024, 1024, own1, out1, recv1a.at[p], sum1a.at[p], recv2a.at[p], sum2a.at[p], recv3a.at[p],
            fin_a.at[p], r1, core * 2048, sums_a.at[p], True)
        for p in range(2)
    ]
    sum_b = [
        Sum(ORDERS[2 - 2 * p], p * 512, 512, own2, out2, recv1b.at[p], sum1b.at[p], recv2b.at[p], None, recv3b.at[p],
            fin_b.at[p], r2, core * 1024, sums_b.at[p], False)
        for p in range(2)
    ]

    def unit(n, length):
        return pl.ds(pl.multiple_of(n * length, length), length)

    def hand1(n):
        rows = unit(n, 256)
        return remote(out1.at[rows], pair1.at[rows], pair1_s.at[n], pair1_r.at[n], partner)

    def hand2(n):
        rows = unit(n, 128)
        return remote(out2.at[rows], pair2.at[rows], pair2_s.at[n], pair2_r.at[n], partner)

    def share(left, right, flip, own, out, at):
        rows = pl.ds(pl.multiple_of(at, 128), 128)
        for which, dst in ((core, own), (1 - core, out)):
            part = mm(left[pl.ds(pl.multiple_of(which * 256, 256), 256), :], right)
            if flip:
                part = part.T
            part = part.astype(dst.dtype)
            dst[rows, 0:256] = part[0:128]
            dst[rows, 256:512] = part[128:256]

    def absorb1(n):
        hand1(n).wait_recv()
        rows = unit(n, 256)
        own1[rows, :] += pair1[rows, :].astype(F32)

    def begin_a(p):
        for n in range(4 * p, 4 * p + 4):
            hand1(n).wait_send()
        sum_a[p].begin()

    wide = 256

    def columns(n):
        cols = pl.ds(pl.multiple_of(n * wide, wide), wide)
        raised = mm(hid[...], w_up[:, cols])
        slope = np.float32(np.sqrt(2 / np.pi))
        square = raised * raised
        t = jnp.tanh(slope * (raised + np.float32(0.044715) * (square * raised)))
        cdf = 0.5 * (1.0 + t)
        activated = (raised * cdf).astype(BF16)
        deriv = cdf + 0.5 * raised * (1.0 - t * t) * (slope * (1.0 + np.float32(3 * 0.044715) * square))
        grad_act = mm_nt(c_ref[...], w_down[cols, :])
        grad_raised = (grad_act * deriv).astype(BF16)
        acc_out[...] += mm(activated, w_down[cols, :])
        acc_in[...] += mm_nt(grad_raised, w_up[:, cols])
        share(hid_t, grad_raised, False, own1, out1, n * 256)
        share(c_t, activated, True, own1, out1, n * 256 + 128)
        hand1(n).start()

        @pl.when(n > 0)
        def _():
            absorb1(n - 1)

        @pl.when(n == 5)
        def _():
            begin_a(0)

    loop(0, FF // wide, columns)
    absorb1(FF // wide - 1)
    begin_a(1)
    gain_part[...] = jnp.zeros_like(gain_part)

    def finish(rows):
        m = mixed[rows, :]
        out_win[rows, :] = (m + acc_out[rows, :]).astype(BF16)
        normed, inv_std = norm_stats(m)
        grad_in = acc_in[rows, :]
        gain_part[1:2, :] += jnp.sum(grad_in * normed, 0, keepdims=True)
        g = c_ref[rows, :].astype(F32) + norm_back(grad_in, normed, inv_std, gain_b)
        acc_in[rows, :] = g
        g = g.astype(BF16)
        hid[rows, :] = g
        g_ctx[rows, :] = mm_nt(g, w_out[...]).astype(BF16)

    rows_loop(TOK, WIN, finish)
    gmix, g_att = acc_in, hid

    hid_t[...] = lowered[...].T
    c_t[...] = context[...].T
    for n in range(2):
        share(c_t, g_att[:, n * 256:(n + 1) * 256], False, own2, out2, (6 + n) * 128)
        hand2(6 + n).start()

    def attend_back(w):
        rows = pl.ds(pl.multiple_of(w * WIN, WIN), WIN)
        bias = window_bias(key_bias[rows, :], split_amount(w))
        for pair in range(4):
            lanes = slice(pair * 128, (pair + 1) * 128)
            key_lanes = slice(D + pair * 128, D + (pair + 1) * 128)
            value_lanes = slice(2 * D + pair * 128, 2 * D + (pair + 1) * 128)
            query = packed[rows, lanes]
            key = packed[rows, key_lanes]
            value = packed[rows, value_lanes]
            grad = g_ctx[rows, lanes]
            sums = [None, None, None]
            for mask in masks:
                query_m = jnp.where(mask, query, 0)
                grad_m = jnp.where(mask, grad, 0)
                probs = scores_t(key, query_m, bias)
                g_weights = mm_nt(value, grad_m)
                inner = jnp.sum(probs * g_weights, 0, keepdims=True)
                g_scores = (probs * (g_weights - inner) * HEAD ** (-0.5)).astype(BF16)
                parts = (
                    mm_tn(g_scores, jnp.where(mask, key, 0)),
                    mm(g_scores, query_m),
                    mm(probs.astype(BF16), grad_m),
                )
                sums = [b if a is None else a + b for a, b in zip(sums, parts)]
            g_pack[rows, lanes] = sums[0].astype(BF16)
            g_pack[rows, key_lanes] = sums[1].astype(BF16)
            g_pack[rows, value_lanes] = sums[2].astype(BF16)
        for when, steps in (
            (0, [sum_a[0].second]),
            (3, [sum_a[1].second, sum_a[0].third]),
            (5, [sum_a[0].gather, sum_a[1].third]),
            (6, [lambda: sum_a[0].gather_next(1), sum_a[1].gather]),
            (7, [lambda: sum_a[0].gather_next(0), lambda: sum_a[1].gather_next(1)]),
        ):
            @pl.when(w == when)
            def _(steps=steps):
                for step in steps:
                    step()

    loop(0, 8, attend_back)
    sum_a[1].gather_next(0)

    def weight(n):
        cols = pl.ds(pl.multiple_of(n * 256, 256), 256)
        share(hid_t, g_pack[:, cols], False, own2, out2, n * 128)
        hand2(n).start()

    loop(0, 6, weight)
    for n in (6, 7, 0, 1, 2, 3, 4, 5):
        hand2(n).wait()
        rows = unit(n, 128)
        own2[rows, :] += pair2[rows, :].astype(F32)
    for part in sum_b:
        part.begin()

    def finish_back(rows):
        g_low = mm_nt(g_pack[rows, :], w_qkv[...]).astype(BF16).astype(F32)
        normed, inv_std = norm_stats(x_ref[rows, :].astype(F32))
        gain_part[0:1, :] += jnp.sum(g_low * normed, 0, keepdims=True)
        gtok_win[rows, :] = (gmix[rows, :] + norm_back(g_low, normed, inv_std, gain_a)).astype(BF16)

    rows_loop(TOK, 288, finish_back)

    gain_slots[0, 0] = gain_part[...]
    gain_pair = remote(gain_slots.at[0, 0], gain_slots.at[0, 1], gain_s.at[0, 0], gain_r.at[0, 0], partner)
    gain_pair.start()
    for k, win in enumerate((out_win, gtok_win)):
        for wr in range(2):
            at = (k * 2 + wr) * 2 * PIECE
            rims[at:at + 2 * PIECE, :] = mm(rim_back[...], win[wr * HALF:(wr + 1) * HALF, :]).astype(BF16)
    halo1 = remote(rims, lon_rims, back_s.at[0], back_r.at[0], (lon_p, lat))
    halo1.start()

    def gains_along(level, total):
        axis = level - 1
        slot = gain_slots.at[level, place[axis]]
        gain_slots[level, place[axis]] = total
        copies = [
            remote(slot, slot, gain_s.at[level, step - 1], gain_r.at[level, step - 1], peer(axis, step))
            for step in (1, 2, 3)
        ]
        for copy in copies:
            copy.start()
        return copies

    def gains_sum(level, copies):
        for copy in copies:
            copy.wait()
        return (gain_slots[level, 0] + gain_slots[level, 1]) + (gain_slots[level, 2] + gain_slots[level, 3])

    for part in sum_b:
        part.second()
    gain_pair.wait()
    gain_copies = gains_along(1, gain_slots[0, 0] + gain_slots[0, 1])
    halo1.wait()
    for k, win in enumerate((out_win, gtok_win)):
        at = (k * 2 + 1) * 2 * PIECE
        for lev in range(2):
            pick = slice(lev * BLOCK, (lev + 1) * BLOCK)
            send_blocks[(k * 2 + lev) * BLOCK:(k * 2 + lev + 1) * BLOCK, :] = (
                mm(back_last[pick, :HALF], win[HALF:, :])
                + mm(back_last[pick, HALF:], lon_rims[at:at + 2 * PIECE, :])
            ).astype(BF16)
    halo2 = remote(send_blocks, lat_blocks, back_s.at[1], back_r.at[1], (lon, lat_p))
    halo2.start()
    for part in sum_a:
        part.gather_pair()
    for part in sum_b:
        part.third()
    gain_copies = gains_along(2, gains_sum(1, gain_copies))
    for part in sum_b:
        part.gather()
    gain_copies = gains_along(3, gains_sum(2, gain_copies))
    for part in sum_b:
        part.gather_next(0)
    gains_out[...] = gains_sum(3, gain_copies) * SCALE
    for part in sum_b:
        part.gather_pair()
    for part in sum_a + sum_b:
        part.end()
    halo2.wait()


def block(*args):
    vm = pl.BlockSpec(memory_space=pltpu.VMEM)
    hbm = pl.BlockSpec(memory_space=pl.ANY)
    shape = jax.ShapeDtypeStruct
    dma = pltpu.SemaphoreType.DMA
    vmem = pltpu.VMEM
    field = vmem((TOK, D), BF16)
    field_t = vmem((D, TOK), BF16)
    wide = vmem((TOK, D), F32)
    rim = vmem((4 * PIECE, D), BF16)
    lat_rim = vmem((2 * BLOCK, D), BF16)
    return pl.pallas_call(
        block_kernel,
        out_shape=(
            shape((2 * FF, D), BF16),
            shape((4 * D, D), BF16),
            shape((8, D), F32),
            shape((TOK, D), BF16),
            shape((TOK, D), BF16),
            shape((8 * PIECE, D), BF16),
            shape((4 * BLOCK, D), BF16),
        ),
        in_specs=[hbm, hbm] + [vm] * 5 + [hbm] * 4 + [vm],
        out_specs=(hbm, hbm) + (vm,) * 5,
        scratch_shapes=[
            vmem((D, 3 * D), BF16), vmem((D, D), BF16), vmem((D, FF), BF16), vmem((FF, D), BF16),
            lat_rim, lat_rim, rim, rim, rim, rim,
            field, field, field, field, field, field_t, field_t, field,
            vmem((TOK, 3 * D), BF16), vmem((TOK, 3 * D), BF16), vmem((HALF + 2 * PIECE, D), BF16),
            wide, wide, wide,
            vmem((FF, D), F32), vmem((FF, D), BF16), vmem((FF, D), BF16),
            vmem((2, 3, 256, D), BF16), vmem((2, 256, D), F32), vmem((2, 3, 64, D), F32), vmem((2, 64, D), F32),
            vmem((2, 3, 16, D), F32), vmem((2, 16, D), BF16),
            vmem((2 * D, D), F32), vmem((2 * D, D), BF16), vmem((2 * D, D), BF16),
            vmem((2, 3, 128, D), BF16), vmem((2, 128, D), F32), vmem((2, 3, 32, D), F32),
            vmem((2, 4, 32, D), F32), vmem((2, 32, D), BF16),
            vmem((8 * PIECE, D), BF16), vmem((4 * BLOCK, D), BF16), vmem((4, 4, 8, D), F32), vmem((8, D), F32),
            dma((6,)), dma((8,)), dma((8,)), dma((2,)), dma((2,)), dma((8,)), dma((8,)), dma((8,)), dma((8,)),
            dma((2, 4, 4, 3)), dma((2, 4, 4, 3)), dma((4, 3)), dma((4, 3)),
        ],
        compiler_params=pltpu.CompilerParams(collective_id=0, has_side_effects=True, vmem_limit_bytes=VMEM_BYTES),
        name="block",
    )(*args)


def finish_kernel(r1, r2, out_win, gtok_win, lon_rims, lat_blocks, back, outputs, g_tok, g_qkv, g_out, g_up, g_down, src):
    for core in range(2):
        for n in range(8):
            for k in range(2):
                lanes = slice(k * 256, (k + 1) * 256)
                rows = slice(core * 256 + k * 128, core * 256 + (k + 1) * 128)
                at = core * 2048 + n * 256
                g_up[rows, n * 256:(n + 1) * 256] = r1[at:at + 128, lanes].astype(F32)
                g_down[n * 256 + k * 128:n * 256 + (k + 1) * 128, core * 256:(core + 1) * 256] = (
                    r1[at + 128:at + 256, lanes].astype(F32)
                )
                at = core * 1024 + n * 128
                if n < 6:
                    g_qkv[rows, n * 256:(n + 1) * 256] = r2[at:at + 128, lanes].astype(F32)
                else:
                    g_out[rows, (n - 6) * 256:(n - 5) * 256] = r2[at:at + 128, lanes].astype(F32)

    for k, (win, full) in enumerate(((out_win, outputs), (gtok_win, g_tok))):
        for wr in range(2):
            at = (k * 2 + wr) * 2 * PIECE
            src[:HALF, :] = win[wr * HALF:(wr + 1) * HALF, :]
            src[HALF:, :] = lon_rims[at:at + 2 * PIECE, :]
            for lev in range(2):
                if wr == 0:
                    pick, length = slice(lev * 288, (lev + 1) * 288), 288
                    to = lev * HALF + 144
                else:
                    pick, length = slice(lev * 288, lev * 288 + 144), 144
                    to = lev * HALF + 432
                full[to:to + length, :] = mm(back[pick, :], src[...]).astype(BF16)
        for lev in range(2):
            full[lev * HALF:lev * HALF + BLOCK, :] = lat_blocks[(k * 2 + lev) * BLOCK:(k * 2 + lev + 1) * BLOCK, :]


def finish_all(*args):
    vm = pl.BlockSpec(memory_space=pltpu.VMEM)
    shape = jax.ShapeDtypeStruct
    return pl.pallas_call(
        finish_kernel,
        out_shape=(
            shape((TOK, D), BF16),
            shape((TOK, D), BF16),
            shape((D, 3 * D), F32),
            shape((D, D), F32),
            shape((D, FF), F32),
            shape((FF, D), F32),
        ),
        in_specs=[vm] * len(args),
        out_specs=(vm,) * 6,
        scratch_shapes=[pltpu.VMEM((HALF + 2 * PIECE, D), BF16)],
        compiler_params=pltpu.CompilerParams(vmem_limit_bytes=VMEM_BYTES),
        name="finish",
    )(*args)


def on_device(tokens, cotangent, valid, w_qkv, w_out, w_up, w_down, gains):
    into, back, rim_in, rim_back = gather_maps()
    tok = tokens.reshape(TOK, D)
    cot = cotangent.reshape(TOK, D)
    usable = jnp.where(valid == 1, 0.0, LOW).astype(F32)
    usable = usable.reshape(2, 12, 4, 6).transpose(0, 2, 1, 3).reshape(8, 1, 72)
    key_bias = jnp.broadcast_to(usable, (8, 2, 72)).reshape(TOK, 1)
    back_last = jnp.concatenate([back[BLOCK:2 * BLOCK], back[3 * BLOCK:]], 0)
    r1, r2, gain_sums, out_win, gtok_win, lon_rims, lat_blocks = block(
        tok, cot, rim_in, into, rim_back, back_last, key_bias, w_qkv, w_out, w_up, w_down, gains
    )
    outputs, g_tok, g_qkv, g_out, g_up, g_down = finish_all(r1, r2, out_win, gtok_win, lon_rims, lat_blocks, back)
    return (
        outputs.reshape(tokens.shape),
        g_tok.reshape(tokens.shape),
        g_qkv,
        g_out,
        g_up,
        g_down,
        gain_sums[:2],
    )


def solution(mesh):
    field = P(None, "lat", "lon", None)
    in_specs = (field, field, P("lat", "lon"), P(), P(), P(), P(), P())
    out_specs = (field, field, P(), P(), P(), P(), P())
    return jax.shard_map(on_device, mesh=mesh, in_specs=in_specs, out_specs=out_specs, check_vma=False)
```

time: 200 us -> 165 us (0.82)
  Pallas kernels: 196 us -> 160 us
    pallas_call x4 -> x1, Pallas kernels: 185 us -> 150 us  [block(): pl.pallas_call(block_kernel, out_shape=(shape((2 * FF, D), BF16), shape((...]
where the time goes in v2:
time: 165 us
  Pallas kernels  160 us (97%)
  local copies, waits for them, and re-layouts  2.74 us (2%)
    pallas_call x1, Pallas kernels, block(): pl.pallas_call(block_kernel, out_shape=(shape((2 * FF, D), BF16), shape((...  150 us
    pallas_call x1, Pallas kernels, finish_all(): pl.pallas_call(finish_kernel, out_shape=(shape((TOK, D), BF16), shape((TO...  10.9 us

profile of v2, /device:TPU:1, one launch (start us, length us, event | category | flops | bytes accessed | tf_op | source)
XLA Modules:
  0.0 164.6 jit_solution(3886258026983518733)
XLA Ops:
  0.6 0.7 compare_select_fusion
  1.3 0.1 copy.19
  1.4 0.1 reshape.36
  1.5 0.1 copy.20
  1.6 0.1 broadcast_in_dim.17
  1.7 1.0 reshape.40.key_bias
  2.8 149.6 %block.1 = (bf16[4096,512]{1,0:T(8,128)(2,1)}, bf16[2048,512]{1,0:T(8,128)(2,1)}, f32[8,512]{1,0:T(8,128)}, bf16[1152,512]{1,0:T(8,128)(2,1)}, bf16[1152,512]{1,...) custom-call(bf16[1152,512]{1,0:T(8,128)(2,1)} %bitcast.7, bf16[1152,512]{1,0:T(8,128)(2,1)} %bitcast.8, ...), custom_call_target="tpu_custom_call" | custom-call | tf_op jit(solution)/shard_map/block/pallas_call | solution.py:625
  152.3 1.3 slice.11
  153.7 10.9 %finish.1 = (bf16[1152,512]{1,0:T(8,128)(2,1)}, bf16[1152,512]{1,0:T(8,128)(2,1)}, f32[512,1536]{1,0:T(8,128)}, f32[512,512]{1,0:T(8,128)}, f32[512,2048]{1,0:T(8,128)}, /*index=5*/f32[2048,512]{1,0:T(8,128)}) custom-call(bf16[4096,512]{1,0:T(8,128)(2,1)} %get-tuple-element.20.r1, bf16[2048,512]{1,0:T(8,128)(2,1)} %get-tuple-element.21.r2, ...), custom_call_target="tpu_custom_call" | custom-call | tf_op jit(solution)/shard_map/finish/pallas_call | solution.py:696
  (1 shorter events, 0.0 us)

commit v3 on v2

v3 whole, which is shorter than its diff:
```python
import jax
import jax.numpy as jnp
import numpy as np
from jax import lax
from jax.experimental import pallas as pl
from jax.experimental.pallas import tpu as pltpu
from jax.sharding import PartitionSpec as P

F32 = jnp.float32
BF16 = jnp.bfloat16
MESH = pl.DeviceIdType.MESH
HEAD = 64
WIN = 144
TOK = 1152
HALF = 576
D = 512
FF = 2048
COLS = 24
BLOCK = 144
PIECE = 48
epsilon = 1e-05
LOW = -1e30
SCALE = np.float32(147456 ** (-0.5))
VMEM_BYTES = 63 * 1024 * 1024


def gather_maps():
    into = np.zeros((HALF, HALF + 2 * PIECE), np.float32)
    back = np.zeros((HALF, HALF + 2 * PIECE), np.float32)
    rim_in = np.zeros((4 * PIECE, TOK), np.float32)
    rim_back = np.zeros((2 * PIECE, HALF), np.float32)
    for lev in range(2):
        for half in range(2):
            for r in range(6):
                for col in range(COLS):
                    window = (col // 6) * WIN + lev * 72 + half * 36 + r * 6 + col % 6
                    chunk = (lev * 2 + half) * BLOCK + r * COLS
                    if col + 3 < COLS:
                        into[window, chunk + col + 3] = 1
                        back[chunk + col + 3, window] = 1
                    else:
                        rim = half * PIECE + lev * 18 + r * 3 + col + 3 - COLS
                        into[window, HALF + rim] = 1
                        back[chunk + col + 3 - COLS, HALF + rim] = 1
                        rim_back[rim, window] = 1
    for lev in range(2):
        for block in range(4):
            for r in range(6):
                for col in range(3):
                    rim_in[block * PIECE + lev * 18 + r * 3 + col, lev * HALF + block * BLOCK + r * COLS + col] = 1
    return [jnp.asarray(m, BF16) for m in (into, back, rim_in, rim_back)]


def mm(a, b):
    return lax.dot_general(a, b, (((1,), (0,)), ((), ())), preferred_element_type=F32)


def mm_nt(a, b):
    return lax.dot_general(a, b, (((1,), (1,)), ((), ())), preferred_element_type=F32)


def mm_tn(a, b):
    return lax.dot_general(a, b, (((0,), (0,)), ((), ())), preferred_element_type=F32)


def norm_stats(values):
    centred = values - jnp.mean(values, -1, keepdims=True)
    inv_std = lax.rsqrt(jnp.mean(centred * centred, -1, keepdims=True) + epsilon)
    return centred * inv_std, inv_std


def norm_back(grad_value, normed, inv_std, gain_row):
    scaled = grad_value * gain_row
    return inv_std * (
        scaled
        - jnp.mean(scaled, -1, keepdims=True)
        - normed * jnp.mean(scaled * normed, -1, keepdims=True)
    )


def rows_loop(total, step, body):
    def run(i, carry):
        body(pl.ds(pl.multiple_of(i * step, step), step))
        return carry

    lax.fori_loop(0, total // step, run, 0)


def window_bias(key_bias, split):
    rows = lax.broadcasted_iota(jnp.int32, (WIN, WIN), 0)
    cols = lax.broadcasted_iota(jnp.int32, (WIN, WIN), 1)
    bias = jnp.where(rows == cols, 0.0, jnp.broadcast_to(key_bias, (WIN, WIN)))
    apart = ((rows // 36) % 2) != ((cols // 36) % 2)
    return bias + jnp.where(apart, split, 0.0)


def scores_t(key2, query_m, bias):
    s = mm_nt(key2, query_m) * HEAD ** (-0.5) + bias
    e = jnp.exp(s - jnp.max(s, 0, keepdims=True))
    return e * (1.0 / jnp.sum(e, 0, keepdims=True))


def head_masks():
    lane = lax.broadcasted_iota(jnp.int32, (WIN, 128), 1)
    return [lane < HEAD, lane >= HEAD]


def split_amount(window):
    last = (lax.axis_index("lat") == lax.axis_size("lat") - 1) & (window >= 4)
    return jnp.where(last, LOW, 0.0).astype(F32)


def position():
    lon, lat = lax.axis_index("lon"), lax.axis_index("lat")
    y = lax.rem(lax.div(lat, 2), 2) * 2 + lax.rem(lon, 2)
    return [lax.div(lon, 2), y, lax.div(lat, 4)], lax.rem(lat, 2)


def device_at(place, core):
    x, y, z = place
    return (x * 2 + lax.rem(y, 2), z * 4 + lax.div(y, 2) * 2 + core)


def remote(src, dst, s, r, device):
    return pltpu.make_async_remote_copy(
        src_ref=src, dst_ref=dst, send_sem=s, recv_sem=r, device_id=device, device_id_type=MESH
    )


def loop(first, last, body):
    def run(i, carry):
        body(i)
        return carry

    lax.fori_loop(first, last, run, 0)


class Sums:
    def __init__(self, own, out, pair, recv1, sum1, recv2, recv3, fin, result, sems, pair_sems):
        self.own, self.out, self.pair = own, out, pair
        self.recv1, self.sum1, self.recv2, self.recv3, self.fin = recv1, sum1, recv2, recv3, fin
        self.result, self.sems, self.pair_sems = result, sems, pair_sems
        self.place, self.core = position()
        self.partner = device_at(self.place, 1 - self.core)
        self.base = self.core * own.shape[0]

    def flags(self, u, level):
        turn = lax.rem(u + level, 3) if not isinstance(u, int) else (u + level) % 3
        first, last = (2 - turn) // 2, turn // 2
        return first, 1 - first - last, last

    def peer(self, u, level, step):
        flags = self.flags(u, level)
        return device_at([lax.rem(at + flag * step, 4) for at, flag in zip(self.place, flags)], self.core)

    def mine(self, u, level):
        x, y, z = (at * flag for at, flag in zip(self.place, self.flags(u, level)))
        return x + y + z

    def rows(self, u):
        return pl.ds(pl.multiple_of(u * 256, 256), 256)

    def rows1(self, u, at):
        return pl.ds(pl.multiple_of(u * 256 + at * 64, 64), 64)

    def result_rows(self, u, level):
        at = self.base + u * 256
        if level < 0:
            return pl.ds(pl.multiple_of(at, 256), 256)
        at = at + self.mine(u, 0) * 64
        if level == 0:
            return pl.ds(pl.multiple_of(at, 64), 64)
        return pl.ds(pl.multiple_of(at + self.mine(u, 1) * 16, 16), 16)

    def down(self, u, level, step):
        s, r = self.sems.at[u, 0, level], self.sems.at[u, 1, level]
        device = self.peer(u, level, step)
        if level == 0:
            there = lax.rem(self.mine(u, 0) + step, 4)
            return remote(self.out.at[self.rows1(u, there)], self.recv1.at[u, step - 1], s, r, device)
        if level == 1:
            there = lax.rem(self.mine(u, 1) + step, 4)
            rows = pl.ds(pl.multiple_of(there * 16, 16), 16)
            return remote(self.sum1.at[u, rows], self.recv2.at[u, step - 1], s, r, device)
        slot = self.recv3.at[u, self.mine(u, 2)]
        return remote(slot, slot, s, r, device)

    def up(self, u, level, step):
        s, r = self.sems.at[u, 2, level], self.sems.at[u, 3, level]
        rows = self.result.at[self.result_rows(u, level)]
        return remote(self.fin.at[u] if level == 1 else rows, rows, s, r, self.peer(u, level, step))

    def hand(self, u):
        rows = self.rows(u)
        return remote(
            self.out.at[rows], self.pair.at[rows], self.pair_sems.at[u, 0], self.pair_sems.at[u, 1], self.partner
        )

    def hand_back(self, u):
        rows = self.result.at[self.result_rows(u, -1)]
        return remote(rows, rows, self.pair_sems.at[u, 2], self.pair_sems.at[u, 3], self.partner)

    def keep(self, u):
        return pltpu.make_async_copy(self.fin.at[u], self.result.at[self.result_rows(u, 1)], self.pair_sems.at[u, 4])

    def done(self, u, kind, level):
        if kind < 2:
            three = (self.recv1.at[u], self.recv2.at[u], self.recv3.at[u, pl.ds(0, 3)])[level]
        else:
            three = (self.recv1.at[u], self.recv1.at[u, 0, pl.ds(0, 48)])[level]
        pltpu.make_async_copy(three, three, self.sems.at[u, kind, level]).wait()

    def send(self, make, u, level):
        for step in (1, 2, 3):
            make(u, level, step).start()

    def begin(self, u):
        self.hand(u).wait()
        rows = self.rows(u)
        total = self.own[rows, :] + self.pair[rows, :].astype(F32)
        self.own[rows, :] = total
        self.out[rows, :] = total.astype(BF16)
        self.send(self.down, u, 0)

    def second(self, u):
        self.done(u, 1, 0)
        rows = self.rows1(u, self.mine(u, 0))
        self.sum1[u] = (self.own[rows, :] + self.recv1[u, 0].astype(F32)) + (
            self.recv1[u, 1].astype(F32) + self.recv1[u, 2].astype(F32)
        )
        self.send(self.down, u, 1)

    def third(self, u):
        self.done(u, 1, 1)
        rows = pl.ds(pl.multiple_of(self.mine(u, 1) * 16, 16), 16)
        self.recv3[u, self.mine(u, 2)] = (self.sum1[u, rows, :] + self.recv2[u, 0]) + (
            self.recv2[u, 1] + self.recv2[u, 2]
        )
        self.send(self.down, u, 2)

    def gather(self, u):
        self.done(u, 1, 2)
        total = (self.recv3[u, 0] + self.recv3[u, 1]) + (self.recv3[u, 2] + self.recv3[u, 3])
        self.fin[u] = (total * SCALE).astype(BF16)
        self.keep(u).start()
        self.send(self.up, u, 1)

    def gather_next(self, u):
        self.keep(u).wait()
        self.done(u, 3, 1)
        self.send(self.up, u, 0)

    def gather_pair(self, u):
        self.done(u, 3, 0)
        self.hand_back(u).start()

    def end(self, u):
        for level in range(3):
            self.done(u, 0, level)
        for level in range(2):
            self.done(u, 2, level)
        self.hand_back(u).wait()

    def stages(self):
        return (self.begin, self.second, self.third, self.gather, self.gather_next, self.gather_pair)


def block_kernel(
    tok, cot, rim_in, into, rim_back, back_last, valid, w_qkv_h, w_out_h, w_up_h, w_down_h, gains,
    r1, r2, r3, gains_out, out_win, gtok_win, lon_rims, lat_blocks,
    w_qkv, w_out, w_up, w_down, lat_t, lat_c, rim_t, rim_c, pack_t, pack_c, key_bias,
    x_ref, c_ref, lowered, context, hid, hid_t, c_t, g_ctx, packed, g_pack, src, mixed, acc_out, acc_in,
    *rest_refs,
):
    place, core = position()
    lon, lat = lax.axis_index("lon"), lax.axis_index("lat")
    n_lon, n_lat = lax.axis_size("lon"), lax.axis_size("lat")
    lon_m, lon_p = lax.rem(lon + n_lon - 1, n_lon), lax.rem(lon + 1, n_lon)
    lat_m, lat_p = lax.rem(lat + n_lat - 1, n_lat), lax.rem(lat + 1, n_lat)
    partner = device_at(place, 1 - core)
    gain_a = gains[0:1, :]
    gain_b = gains[1:2, :]
    masks = head_masks()
    refs = iter(rest_refs)
    results = (r1, r2, r3)
    sum_a, sum_b, sum_c = (
        Sums(*[next(refs) for _ in range(8)], results[k], next(refs), next(refs)) for k in range(3)
    )
    (rims, send_blocks, gain_slots, gain_part,
     load_sem, halo_s, halo_r, back_s, back_r, gain_s, gain_r) = refs

    def peer(axis, step):
        there = list(place)
        there[axis] = lax.rem(place[axis] + step, 4)
        return device_at(there, core)

    barrier = pltpu.get_barrier_semaphore()
    greet = [(lon, lat_m), (lon, lat_p), (lon_m, lat), (lon_p, lat), (lon_m, lat_m), (lon_p, lat_p), partner]
    greet += [peer(axis, step) for axis in range(3) for step in (1, 2, 3)]
    for device in greet:
        pl.semaphore_signal(barrier, inc=1, device_id=device, device_id_type=MESH)
    loads = [
        pltpu.make_async_copy(a, b, load_sem.at[k])
        for k, (a, b) in enumerate(
            ((tok, context), (cot, out_win), (w_out_h, w_out), (w_up_h, w_up), (w_down_h, w_down))
        )
    ]
    loads += [
        pltpu.make_async_copy(
            w_qkv_h.at[:, pl.ds(part * D + pair * 128, 128)],
            w_qkv.at[:, pl.ds(pair * 384 + part * 128, 128)],
            load_sem.at[5 + part * 4 + pair],
        )
        for part in range(3)
        for pair in range(4)
    ]
    for copy in loads:
        copy.start()
    loads[0].wait()
    pack_t[...] = mm(rim_in[...], context[...]).astype(BF16)
    pl.semaphore_wait(barrier, len(greet))

    halos = []
    rest = pl.ds(PIECE, 3 * PIECE)
    corner = pl.ds(0, PIECE)

    def send_halos(pack, rim, lat_rim, full):
        wanted = [
            (pack.at[rest], rim.at[rest], (lon_m, lat)),
            (pack.at[corner], rim.at[corner], (lon_m, lat_m)),
        ]
        for lev in range(2):
            wanted.append(
                (full.at[pl.ds(lev * HALF, BLOCK)], lat_rim.at[pl.ds(lev * BLOCK, BLOCK)], (lon, lat_m))
            )
        for a, b, device in wanted:
            k = len(halos)
            halos.append(remote(a, b, halo_s.at[k], halo_r.at[k], device))
            halos[k].start()

    send_halos(pack_t, rim_t, lat_t, context)
    usable = jnp.where(valid[...] == 1, 1.0, 0.0).astype(BF16)
    spot = lax.broadcasted_iota(jnp.int32, (WIN, COLS), 0)
    lane = lax.broadcasted_iota(jnp.int32, (WIN, COLS), 1)
    for wr in range(2):
        lat_at = wr * 12 + ((spot // 36) % 2) * 6 + (spot // 6) % 6
        picked = mm(jnp.where(lane == lat_at, 1.0, 0.0).astype(BF16), usable)
        for k in range(4):
            ok = jnp.sum(jnp.where(lane == 6 * k + spot % 6, picked, 0.0), 1, keepdims=True)
            key_bias[(wr * 4 + k) * WIN:(wr * 4 + k + 1) * WIN, :] = jnp.where(ok > 0.5, 0.0, LOW)

    def own_rows(full, wr):
        for lev in range(2):
            if wr == 0:
                src[lev * 288:(lev + 1) * 288, :] = full[lev * HALF + 144:lev * HALF + 432, :]
            else:
                src[lev * 288:lev * 288 + 144, :] = full[lev * HALF + 432:lev * HALF + 576, :]

    def rim_rows(lat_rim, rim, wr):
        if wr == 0:
            src[HALF:, :] = rim[PIECE:3 * PIECE, :]
        else:
            for lev in range(2):
                src[lev * 288 + 144:(lev + 1) * 288, :] = lat_rim[lev * BLOCK:(lev + 1) * BLOCK, :]
            src[HALF:HALF + PIECE, :] = rim[3 * PIECE:, :]
            src[HALF + PIECE:, :] = rim[:PIECE, :]

    def enter(dst, wr, first, last, depth):
        for n in range(2):
            cols = slice(n * 256, (n + 1) * 256)
            dst[wr * HALF + first:wr * HALF + last, cols] = mm(into[first:last, :depth], src[:depth, cols]).astype(BF16)

    def attend(w):
        rows = pl.ds(pl.multiple_of(w * WIN, WIN), WIN)
        bias = window_bias(key_bias[rows, :], split_amount(w))
        for pair in range(4):
            lanes = slice(pair * 128, (pair + 1) * 128)
            query, key, value = (packed[rows, pair * 384 + k * 128:pair * 384 + (k + 1) * 128] for k in range(3))
            total = None
            for mask in masks:
                probs = scores_t(key, jnp.where(mask, query, 0), bias)
                part = mm_tn(probs.astype(BF16), jnp.where(mask, value, 0))
                total = part if total is None else total + part
            hid[rows, lanes] = total.astype(BF16)

    def first_part(first, last):
        band = slice(first * WIN, last * WIN)

        def first_norm(i):
            rows = pl.ds(pl.multiple_of(i * WIN, WIN), WIN)
            normed, _ = norm_stats(x_ref[rows, :].astype(F32))
            lowered[rows, :] = (normed * gain_a).astype(BF16)

        loop(first, last, first_norm)

        def project(n):
            cols = pl.ds(pl.multiple_of(n * 256, 256), 256)
            packed[band, cols] = mm(lowered[band, :], w_qkv[:, cols]).astype(BF16)

        loop(0, 6, project)
        loop(first, last, attend)

    own_rows(context, 0)
    enter(x_ref, 0, 0, 3 * WIN, HALF)
    for copy in loads[5:]:
        copy.wait()
    first_part(0, 3)
    loads[1].wait()
    pack_c[...] = mm(rim_in[...], out_win[...]).astype(BF16)
    send_halos(pack_c, rim_c, lat_c, out_win)
    for copy in halos[0:4]:
        copy.wait_recv()
    rim_rows(lat_t, rim_t, 0)
    enter(x_ref, 0, 3 * WIN, HALF, HALF + 2 * PIECE)
    own_rows(context, 1)
    rim_rows(lat_t, rim_t, 1)
    enter(x_ref, 1, 0, HALF, HALF + 2 * PIECE)
    first_part(3, 8)
    for copy in halos[4:8]:
        copy.wait_recv()
    for wr in range(2):
        own_rows(out_win, wr)
        rim_rows(lat_c, rim_c, wr)
        enter(c_ref, wr, 0, HALF, HALF + 2 * PIECE)
    for copy in halos:
        copy.wait_send()
    loads[2].wait()
    context[...] = hid[...]

    def second_norm(rows):
        attended = mm(context[rows, :], w_out[...]).astype(BF16)
        m = x_ref[rows, :].astype(F32) + attended.astype(F32)
        mixed[rows, :] = m
        normed, _ = norm_stats(m)
        hid[rows, :] = (normed * gain_b).astype(BF16)

    rows_loop(TOK, 288, second_norm)
    hid_t[...] = hid[...].T
    c_t[...] = c_ref[...].T
    acc_out[...] = jnp.zeros_like(acc_out)
    acc_in[...] = jnp.zeros_like(acc_in)
    loads[3].wait()
    loads[4].wait()

    def tick(t):
        for stage, lag in reversed(list(zip(sum_a.stages(), LAGS))):
            u = t - lag
            if isinstance(t, int):
                if 0 <= u < 8:
                    stage(u)
            else:
                @pl.when((u >= 0) & (u < 8))
                def _(stage=stage, u=u):
                    stage(u)

    def share(left, right, flip, own, out, at):
        rows = pl.ds(pl.multiple_of(at, 128), 128)
        for which, dst in ((core, own), (1 - core, out)):
            part = mm(left[pl.ds(pl.multiple_of(which * 256, 256), 256), :], right)
            if flip:
                part = part.T
            part = part.astype(dst.dtype)
            dst[rows, 0:256] = part[0:128]
            dst[rows, 256:512] = part[128:256]

    wide = 256

    def columns(n):
        cols = pl.ds(pl.multiple_of(n * wide, wide), wide)
        raised = mm(hid[...], w_up[:, cols])
        slope = np.float32(np.sqrt(2 / np.pi))
        square = raised * raised
        t = jnp.tanh(slope * (raised + np.float32(0.044715) * (square * raised)))
        cdf = 0.5 * (1.0 + t)
        activated = (raised * cdf).astype(BF16)
        deriv = cdf + 0.5 * raised * (1.0 - t * t) * (slope * (1.0 + np.float32(3 * 0.044715) * square))
        grad_act = mm_nt(c_ref[...], w_down[cols, :])
        grad_raised = (grad_act * deriv).astype(BF16)
        acc_out[...] += mm(activated, w_down[cols, :])
        acc_in[...] += mm_nt(grad_raised, w_up[:, cols])
        share(hid_t, grad_raised, False, sum_a.own, sum_a.out, n * 256)
        share(c_t, activated, True, sum_a.own, sum_a.out, n * 256 + 128)
        sum_a.hand(n).start()
        tick(n)

    loop(0, FF // wide, columns)
    tick(8)
    gain_part[...] = jnp.zeros_like(gain_part)

    def finish(rows):
        m = mixed[rows, :]
        out_win[rows, :] = (m + acc_out[rows, :]).astype(BF16)
        normed, inv_std = norm_stats(m)
        grad_in = acc_in[rows, :]
        gain_part[1:2, :] += jnp.sum(grad_in * normed, 0, keepdims=True)
        g = c_ref[rows, :].astype(F32) + norm_back(grad_in, normed, inv_std, gain_b)
        acc_in[rows, :] = g
        g = g.astype(BF16)
        hid[rows, :] = g
        g_ctx[rows, :] = mm_nt(g, w_out[...]).astype(BF16)

    rows_loop(TOK, WIN, finish)
    backs = []

    def send_back(k, win):
        for wr in range(2):
            at = (k * 2 + wr) * 2 * PIECE
            rims[at:at + 2 * PIECE, :] = mm(rim_back[...], win[wr * HALF:(wr + 1) * HALF, :]).astype(BF16)
        send_blocks[k * 2 * BLOCK:(k + 1) * 2 * BLOCK, :] = mm(back_last[...], win[HALF:, :]).astype(BF16)
        near = pl.ds(k * 4 * PIECE, 3 * PIECE)
        far = pl.ds(k * 4 * PIECE + 3 * PIECE, PIECE)
        blocks = pl.ds(k * 2 * BLOCK, 2 * BLOCK)
        for a, b, device in (
            (send_blocks.at[blocks], lat_blocks.at[blocks], (lon, lat_p)),
            (rims.at[near], lon_rims.at[near], (lon_p, lat)),
            (rims.at[far], lon_rims.at[far], (lon_p, lat_p)),
        ):
            n = len(backs)
            backs.append(remote(a, b, back_s.at[n], back_r.at[n], device))
            backs[n].start()

    send_back(0, out_win)
    gmix, g_att = acc_in, hid

    tick(9)
    hid_t[...] = lowered[...].T
    c_t[...] = context[...].T
    for which, dst in ((core, sum_c.own), (1 - core, sum_c.out)):
        part = mm(c_t[pl.ds(pl.multiple_of(which * 256, 256), 256), :], g_att[...])
        dst[...] = part.astype(dst.dtype)
    sum_c.hand(0).start()
    tick(10)

    def attend_back(w, pair):
        rows = pl.ds(pl.multiple_of(w * WIN, WIN), WIN)
        bias = window_bias(key_bias[rows, :], split_amount(w))
        lanes = [pl.ds(pl.multiple_of(pair * 384 + k * 128, 128), 128) for k in range(3)]
        query, key, value = (packed[rows, at] for at in lanes)
        grad = g_ctx[rows, pl.ds(pl.multiple_of(pair * 128, 128), 128)]
        sums = [None, None, None]
        for mask in masks:
            query_m = jnp.where(mask, query, 0)
            grad_m = jnp.where(mask, grad, 0)
            probs = scores_t(key, query_m, bias)
            g_weights = mm_nt(value, grad_m)
            inner = jnp.sum(probs * g_weights, 0, keepdims=True)
            g_scores = (probs * (g_weights - inner) * HEAD ** (-0.5)).astype(BF16)
            parts = (
                mm_tn(g_scores, jnp.where(mask, key, 0)),
                mm(g_scores, query_m),
                mm(probs.astype(BF16), grad_m),
            )
            sums = [b if a is None else a + b for a, b in zip(sums, parts)]
        for at, value in zip(lanes, sums):
            g_pack[rows, at] = value.astype(BF16)

    both = (sum_b, sum_c)

    def heads(pair):
        def some(k):
            for w in range(4):
                attend_back(k * 4 + w, pair)
            now = 2 * pair + k
            for when, which, stage, u in LATE:
                @pl.when(now == when)
                def _(which=which, stage=stage, u=u):
                    both[which].stages()[stage](u)

            tick(11 + now)

        loop(0, 2, some)
        cols = pl.ds(pl.multiple_of(pair * 384, 384), 384)
        rows = pl.ds(pl.multiple_of(pair * 256, 256), 256)
        for which, dst in ((core, sum_b.own), (1 - core, sum_b.out)):
            part = mm(hid_t[pl.ds(pl.multiple_of(which * 256, 256), 256), :], g_pack[:, cols])
            dst[rows, :] = part.astype(dst.dtype)
        sum_b.hand(pair).start()

    loop(0, 4, heads)
    tick(19)

    def finish_back(rows):
        g_low = mm_nt(g_pack[rows, :], w_qkv[...]).astype(BF16).astype(F32)
        normed, inv_std = norm_stats(x_ref[rows, :].astype(F32))
        gain_part[0:1, :] += jnp.sum(g_low * normed, 0, keepdims=True)
        gtok_win[rows, :] = (gmix[rows, :] + norm_back(g_low, normed, inv_std, gain_a)).astype(BF16)

    def later(phase):
        for which, stage, u in PHASES[phase]:
            both[which].stages()[stage](u)

    rows_loop(TOK // 2, 288, finish_back)
    later(0)
    tick(20)
    rows_loop(TOK // 2, 288, lambda rows: finish_back(pl.ds(pl.multiple_of(rows.start + TOK // 2, 288), 288)))
    send_back(1, gtok_win)
    later(1)
    tick(21)
    gain_slots[0, 0] = gain_part[...]
    gain_pair = remote(gain_slots.at[0, 0], gain_slots.at[0, 1], gain_s.at[0, 0], gain_r.at[0, 0], partner)
    gain_pair.start()
    def gains_along(level, total):
        axis = level - 1
        slot = gain_slots.at[level, place[axis]]
        gain_slots[level, place[axis]] = total
        copies = [
            remote(slot, slot, gain_s.at[level, step - 1], gain_r.at[level, step - 1], peer(axis, step))
            for step in (1, 2, 3)
        ]
        for copy in copies:
            copy.start()
        return copies

    def gains_sum(level, copies):
        for copy in copies:
            copy.wait()
        return (gain_slots[level, 0] + gain_slots[level, 1]) + (gain_slots[level, 2] + gain_slots[level, 3])

    gain_pair.wait()
    gain_copies = gains_along(1, gain_slots[0, 0] + gain_slots[0, 1])
    later(2)
    gain_copies = gains_along(2, gains_sum(1, gain_copies))
    later(3)
    gain_copies = gains_along(3, gains_sum(2, gain_copies))
    later(4)
    gains_out[...] = gains_sum(3, gain_copies) * SCALE
    later(5)
    loop(0, 8, sum_a.end)
    sum_c.end(0)
    loop(0, 4, sum_b.end)
    for copy in backs:
        copy.wait()


LAGS = (1, 4, 6, 8, 10, 13)
LATE = (
    (0, 1, 0, 0), (2, 1, 1, 0), (4, 1, 2, 0), (6, 1, 3, 0),
    (6, 0, 2, 0), (4, 0, 1, 0), (2, 0, 0, 0), (6, 0, 1, 1), (4, 0, 0, 1), (6, 0, 0, 2),
)
PHASES = (
    ((1, 4, 0), (0, 3, 0), (0, 2, 1), (0, 1, 2), (0, 0, 3)),
    ((1, 5, 0), (0, 4, 0), (0, 3, 1), (0, 2, 2), (0, 1, 3)),
    ((0, 5, 0), (0, 4, 1), (0, 3, 2), (0, 2, 3)),
    ((0, 5, 1), (0, 4, 2), (0, 3, 3)),
    ((0, 5, 2), (0, 4, 3)),
    ((0, 5, 3),),
)


def sums_scratch(units, lanes):
    vmem = pltpu.VMEM
    return [
        vmem((units * 256, lanes), F32), vmem((units * 256, lanes), BF16), vmem((units * 256, lanes), BF16),
        vmem((units, 3, 64, lanes), BF16), vmem((units, 64, lanes), F32), vmem((units, 3, 16, lanes), F32),
        vmem((units, 4, 16, lanes), F32), vmem((units, 16, lanes), BF16),
        pltpu.SemaphoreType.DMA((units, 4, 3)), pltpu.SemaphoreType.DMA((units, 5)),
    ]


def block(*args):
    vm = pl.BlockSpec(memory_space=pltpu.VMEM)
    hbm = pl.BlockSpec(memory_space=pl.ANY)
    shape = jax.ShapeDtypeStruct
    dma = pltpu.SemaphoreType.DMA
    vmem = pltpu.VMEM
    field = vmem((TOK, D), BF16)
    field_t = vmem((D, TOK), BF16)
    wide = vmem((TOK, D), F32)
    rim = vmem((4 * PIECE, D), BF16)
    lat_rim = vmem((2 * BLOCK, D), BF16)
    return pl.pallas_call(
        block_kernel,
        out_shape=(
            shape((2 * FF, D), BF16),
            shape((4 * D, 384), BF16),
            shape((D, D), BF16),
            shape((8, D), F32),
            shape((TOK, D), BF16),
            shape((TOK, D), BF16),
            shape((8 * PIECE, D), BF16),
            shape((4 * BLOCK, D), BF16),
        ),
        in_specs=[hbm, hbm] + [vm] * 5 + [hbm] * 4 + [vm],
        out_specs=(hbm,) * 3 + (vm,) * 5,
        scratch_shapes=[
            vmem((D, 3 * D), BF16), vmem((D, D), BF16), vmem((D, FF), BF16), vmem((FF, D), BF16),
            lat_rim, lat_rim, rim, rim, rim, rim, vmem((TOK, 1), F32),
            field, field, field, field, field, field_t, field_t, field,
            vmem((TOK, 3 * D), BF16), vmem((TOK, 3 * D), BF16), vmem((HALF + 2 * PIECE, D), BF16),
            wide, wide, wide,
            *sums_scratch(8, D), *sums_scratch(4, 384), *sums_scratch(1, D),
            vmem((8 * PIECE, D), BF16), vmem((4 * BLOCK, D), BF16), vmem((4, 4, 8, D), F32), vmem((8, D), F32),
            dma((17,)), dma((8,)), dma((8,)), dma((6,)), dma((6,)), dma((4, 3)), dma((4, 3)),
        ],
        compiler_params=pltpu.CompilerParams(collective_id=0, has_side_effects=True, vmem_limit_bytes=VMEM_BYTES),
        name="block",
    )(*args)


def finish_kernel(
    r1, r2, r3, gain_sums, out_win, gtok_win, lon_rims, lat_blocks, back,
    outputs, g_tok, g_qkv, g_out, g_up, g_down, g_gains,
    v1, v2, v3, w1, w2, rims, blocks, src, full, f_up, f_down, f_qkv, f_out, sem_in, sem_out,
):
    loads = [
        pltpu.make_async_copy(a, b, sem_in.at[k])
        for k, (a, b) in enumerate(
            [(r1.at[pl.ds(core * FF + n * 1024, 1024)], v1.at[pl.ds(core * FF + n * 1024, 1024)])
             for n in range(2) for core in range(2)]
            + [(r2, v2), (r3, v3), (out_win, w1), (lon_rims, rims), (lat_blocks, blocks), (gtok_win, w2)]
        )
    ]
    for copy in loads:
        copy.start()
    stores = []

    def store(a, b):
        copy = pltpu.make_async_copy(a, b, sem_out.at[len(stores)])
        copy.start()
        stores.append(copy)

    g_gains[...] = gain_sums[0:2, :]
    for n in range(8):
        if n % 4 == 0:
            loads[n // 2].wait()
            loads[n // 2 + 1].wait()
        for core in range(2):
            for k in range(2):
                lanes = slice(k * 256, (k + 1) * 256)
                at = core * FF + n * 256
                f_up[core * 256 + k * 128:core * 256 + (k + 1) * 128, n * 256:(n + 1) * 256] = (
                    v1[at:at + 128, lanes].astype(F32)
                )
                f_down[n * 256 + k * 128:n * 256 + (k + 1) * 128, core * 256:(core + 1) * 256] = (
                    v1[at + 128:at + 256, lanes].astype(F32)
                )
        if n % 2:
            cols = pl.ds((n - 1) * 256, 512)
            store(f_up.at[:, cols], g_up.at[:, cols])
            store(f_down.at[cols], g_down.at[cols])
    loads[4].wait()
    for part in range(3):
        for pair in range(4):
            for core in range(2):
                f_qkv[core * 256:(core + 1) * 256, part * D + pair * 128:part * D + (pair + 1) * 128] = (
                    v2[core * 1024 + pair * 256:core * 1024 + (pair + 1) * 256, part * 128:(part + 1) * 128].astype(F32)
                )
        cols = pl.ds(part * D, D)
        store(f_qkv.at[:, cols], g_qkv.at[:, cols])
    loads[5].wait()
    f_out[...] = v3[...].astype(F32)
    store(f_out, g_out)
    for copy in loads[6:]:
        copy.wait()
    for k, (win, out) in enumerate(((w1, outputs), (w2, g_tok))):
        for wr in range(2):
            at = (k * 2 + wr) * 2 * PIECE
            src[:HALF, :] = win[wr * HALF:(wr + 1) * HALF, :]
            src[HALF:, :] = rims[at:at + 2 * PIECE, :]
            for lev in range(2):
                if wr == 0:
                    pick, length = slice(lev * 288, (lev + 1) * 288), 288
                    to = lev * HALF + 144
                else:
                    pick, length = slice(lev * 288, lev * 288 + 144), 144
                    to = lev * HALF + 432
                full[k, to:to + length, :] = mm(back[pick, :], src[...]).astype(BF16)
        for lev in range(2):
            edge = mm(back[lev * 288 + BLOCK:(lev + 1) * 288, HALF:], src[HALF:, :])
            inner = blocks[(k * 2 + lev) * BLOCK:(k * 2 + lev + 1) * BLOCK, :].astype(F32)
            full[k, lev * HALF:lev * HALF + BLOCK, :] = (inner + edge).astype(BF16)
        store(full.at[k], out)
    for copy in stores:
        copy.wait()


def finish_all(*args):
    vm = pl.BlockSpec(memory_space=pltpu.VMEM)
    hbm = pl.BlockSpec(memory_space=pl.ANY)
    shape = jax.ShapeDtypeStruct
    vmem = pltpu.VMEM
    return pl.pallas_call(
        finish_kernel,
        out_shape=(
            shape((TOK, D), BF16),
            shape((TOK, D), BF16),
            shape((D, 3 * D), F32),
            shape((D, D), F32),
            shape((D, FF), F32),
            shape((FF, D), F32),
            shape((2, D), F32),
        ),
        in_specs=[hbm] * 3 + [vm] + [hbm] * 4 + [vm],
        out_specs=(hbm,) * 6 + (vm,),
        scratch_shapes=[
            vmem((2 * FF, D), BF16), vmem((4 * D, 384), BF16), vmem((D, D), BF16), vmem((TOK, D), BF16),
            vmem((TOK, D), BF16), vmem((8 * PIECE, D), BF16), vmem((4 * BLOCK, D), BF16),
            vmem((HALF + 2 * PIECE, D), BF16), vmem((2, TOK, D), BF16),
            vmem((D, FF), F32), vmem((FF, D), F32), vmem((D, 3 * D), F32), vmem((D, D), F32),
            pltpu.SemaphoreType.DMA((10,)), pltpu.SemaphoreType.DMA((14,)),
        ],
        compiler_params=pltpu.CompilerParams(vmem_limit_bytes=VMEM_BYTES),
        name="finish",
    )(*args)


def on_device(tokens, cotangent, valid, w_qkv, w_out, w_up, w_down, gains):
    into, back, rim_in, rim_back = gather_maps()
    tok = tokens.reshape(TOK, D)
    cot = cotangent.reshape(TOK, D)
    back_last = jnp.concatenate([back[BLOCK:2 * BLOCK, :HALF], back[3 * BLOCK:, :HALF]], 0)
    *sums, out_win, gtok_win, lon_rims, lat_blocks = block(
        tok, cot, rim_in, into, rim_back, back_last, valid, w_qkv, w_out, w_up, w_down, gains
    )
    outputs, g_tok, g_qkv, g_out, g_up, g_down, g_gains = finish_all(
        *sums, out_win, gtok_win, lon_rims, lat_blocks, back
    )
    return (
        outputs.reshape(tokens.shape),
        g_tok.reshape(tokens.shape),
        g_qkv,
        g_out,
        g_up,
        g_down,
        g_gains,
    )


def solution(mesh):
    field = P(None, "lat", "lon", None)
    in_specs = (field, field, P("lat", "lon"), P(), P(), P(), P(), P())
    out_specs = (field, field, P(), P(), P(), P(), P())
    return jax.shard_map(on_device, mesh=mesh, in_specs=in_specs, out_specs=out_specs, check_vma=False)
```

time: 165 us -> 148 us (0.90)
  Pallas kernels: 160 us -> 147 us
  local copies, waits for them, and re-layouts: 2.74 us -> 0 us
    pallas_call x1, Pallas kernels: 150 us -> 135 us  [block(): pl.pallas_call(block_kernel, out_shape=(shape((2 * FF, D), BF16), shape((...]
where the time goes in v3:
time: 148 us; the launch traced here: 147 us
  Pallas kernels  147 us (99%)
    pallas_call x1, Pallas kernels, block(): pl.pallas_call(block_kernel, out_shape=(shape((2 * FF, D), BF16), shape((...  135 us
    pallas_call x1, Pallas kernels, finish_all(): pl.pallas_call(finish_kernel, out_shape=(shape((TOK, D), BF16), shape((TO...  11.4 us

profile of v3, /device:TPU:1, one launch (start us, length us, event | category | flops | bytes accessed | tf_op | source)
XLA Modules:
  0.0 147.5 jit_solution(6055239326105163909)
XLA Ops:
  0.6 135.3 %block.1 = (bf16[4096,512]{1,0:T(8,128)(2,1)}, bf16[2048,384]{1,0:T(8,128)(2,1)}, bf16[512,512]{1,0:T(8,128)(2,1)}, f32[8,512]{1,0:T(8,128)}, bf16[1152,512]{1,0...) custom-call(bf16[1152,512]{1,0:T(8,128)(2,1)} %bitcast.4, ...), custom_call_target="tpu_custom_call" | custom-call | tf_op jit(solution)/shard_map/block/pallas_call | solution.py:671
  136.0 11.4 %finish.1 = (bf16[1152,512]{1,0:T(8,128)(2,1)}, bf16[1152,512]{1,0:T(8,128)(2,1)}, f32[512,1536]{1,0:T(8,128)}, f32[512,512]{1,0:T(8,128)}, f32[512,2048]{1,0:T(...) custom-call(bf16[4096,512]{1,0:T(8,128)(2,1)} %get-tuple-element.22.r1, bf16[2048,384]{1,0:T(8,128)(2,1)} %get-tuple-element.23.r2, ...), custom_call_target="tpu_custom_call" | custom-call | tf_op jit(solution)/shard_map/finish/pallas_call | solution.py:782

commit v4 on v3

--- a/solution.py
+++ b/solution.py
@@ -95,9 +95,7 @@
 
 
 def scores_t(key2, query_m, bias):
-    s = mm_nt(key2, query_m) * HEAD ** (-0.5) + bias
-    e = jnp.exp(s - jnp.max(s, 0, keepdims=True))
-    return e * (1.0 / jnp.sum(e, 0, keepdims=True))
+    return mm_nt(key2, query_m) + bias
 
 
 def head_masks():
@@ -268,7 +266,7 @@
 def block_kernel(
     tok, cot, rim_in, into, rim_back, back_last, valid, w_qkv_h, w_out_h, w_up_h, w_down_h, gains,
     r1, r2, r3, gains_out, out_win, gtok_win, lon_rims, lat_blocks,
-    w_qkv, w_out, w_up, w_down, lat_t, lat_c, rim_t, rim_c, pack_t, pack_c, key_bias,
+    w_qkv, w_out, w_up, w_down, lat_t, lat_c, rim_t, rim_c, pack_t, pack_c, key_bias, log_sum,
     x_ref, c_ref, lowered, context, hid, hid_t, c_t, g_ctx, packed, g_pack, src, mixed, acc_out, acc_in,
     *rest_refs,
 ):
@@ -377,8 +375,13 @@
             lanes = slice(pair * 128, (pair + 1) * 128)
             query, key, value = (packed[rows, pair * 384 + k * 128:pair * 384 + (k + 1) * 128] for k in range(3))
             total = None
-            for mask in masks:
-                probs = scores_t(key, jnp.where(mask, query, 0), bias)
+            for half, mask in enumerate(masks):
+                scores = scores_t(key, jnp.where(mask, query, 0), bias)
+                largest = jnp.max(scores, 0, keepdims=True)
+                probs = jnp.exp(scores - largest)
+                total_e = jnp.sum(probs, 0, keepdims=True)
+                probs = probs * (1.0 / total_e)
+                log_sum[pl.ds(w * 8 + pair * 2 + half, 1), :] = largest + jnp.log(total_e)
                 part = mm_tn(probs.astype(BF16), jnp.where(mask, value, 0))
                 total = part if total is None else total + part
             hid[rows, lanes] = total.astype(BF16)
@@ -395,7 +398,9 @@
 
         def project(n):
             cols = pl.ds(pl.multiple_of(n * 256, 256), 256)
-            packed[band, cols] = mm(lowered[band, :], w_qkv[:, cols]).astype(BF16)
+            lane = n * 256 + lax.broadcasted_iota(jnp.int32, (1, 256), 1)
+            factor = jnp.where(lax.rem(lane, 384) < 128, HEAD ** (-0.5), 1.0)
+            packed[band, cols] = (mm(lowered[band, :], w_qkv[:, cols]) * factor).astype(BF16)
 
         loop(0, 6, project)
         loop(first, last, attend)
@@ -538,19 +543,20 @@
         query, key, value = (packed[rows, at] for at in lanes)
         grad = g_ctx[rows, pl.ds(pl.multiple_of(pair * 128, 128), 128)]
         sums = [None, None, None]
-        for mask in masks:
+        for half, mask in enumerate(masks):
             query_m = jnp.where(mask, query, 0)
             grad_m = jnp.where(mask, grad, 0)
-            probs = scores_t(key, query_m, bias)
+            probs = jnp.exp(scores_t(key, query_m, bias) - log_sum[pl.ds(w * 8 + pair * 2 + half, 1), :])
             g_weights = mm_nt(value, grad_m)
             inner = jnp.sum(probs * g_weights, 0, keepdims=True)
-            g_scores = (probs * (g_weights - inner) * HEAD ** (-0.5)).astype(BF16)
+            g_scores = (probs * (g_weights - inner)).astype(BF16)
             parts = (
                 mm_tn(g_scores, jnp.where(mask, key, 0)),
                 mm(g_scores, query_m),
                 mm(probs.astype(BF16), grad_m),
             )
             sums = [b if a is None else a + b for a, b in zip(sums, parts)]
+        sums[0] = sums[0] * HEAD ** (-0.5)
         for at, value in zip(lanes, sums):
             g_pack[rows, at] = value.astype(BF16)
 
@@ -571,10 +577,11 @@
         loop(0, 2, some)
         cols = pl.ds(pl.multiple_of(pair * 384, 384), 384)
         rows = pl.ds(pl.multiple_of(pair * 256, 256), 256)
-        for which, dst in ((core, sum_b.own), (1 - core, sum_b.out)):
+        for which, dst in ((1 - core, sum_b.out), (core, sum_b.own)):
             part = mm(hid_t[pl.ds(pl.multiple_of(which * 256, 256), 256), :], g_pack[:, cols])
             dst[rows, :] = part.astype(dst.dtype)
-        sum_b.hand(pair).start()
+            if dst is sum_b.out:
+                sum_b.hand(pair).start()
 
     loop(0, 4, heads)
     tick(19)
@@ -619,8 +626,10 @@
     gain_pair.wait()
     gain_copies = gains_along(1, gain_slots[0, 0] + gain_slots[0, 1])
     later(2)
+    tick(22)
     gain_copies = gains_along(2, gains_sum(1, gain_copies))
     later(3)
+    tick(23)
     gain_copies = gains_along(3, gains_sum(2, gain_copies))
     later(4)
     gains_out[...] = gains_sum(3, gain_copies) * SCALE
@@ -632,7 +641,7 @@
         copy.wait()
 
 
-LAGS = (1, 4, 6, 8, 10, 13)
+LAGS = (1, 4, 7, 10, 13, 16)
 LATE = (
     (0, 1, 0, 0), (2, 1, 1, 0), (4, 1, 2, 0), (6, 1, 3, 0),
     (6, 0, 2, 0), (4, 0, 1, 0), (2, 0, 0, 0), (6, 0, 1, 1), (4, 0, 0, 1), (6, 0, 0, 2),
@@ -684,7 +693,7 @@
         out_specs=(hbm,) * 3 + (vm,) * 5,
         scratch_shapes=[
             vmem((D, 3 * D), BF16), vmem((D, D), BF16), vmem((D, FF), BF16), vmem((FF, D), BF16),
-            lat_rim, lat_rim, rim, rim, rim, rim, vmem((TOK, 1), F32),
+            lat_rim, lat_rim, rim, rim, rim, rim, vmem((TOK, 1), F32), vmem((64, WIN), F32),
             field, field, field, field, field, field_t, field_t, field,
             vmem((TOK, 3 * D), BF16), vmem((TOK, 3 * D), BF16), vmem((HALF + 2 * PIECE, D), BF16),
             wide, wide, wide,
@@ -702,14 +711,13 @@
     outputs, g_tok, g_qkv, g_out, g_up, g_down, g_gains,
     v1, v2, v3, w1, w2, rims, blocks, src, full, f_up, f_down, f_qkv, f_out, sem_in, sem_out,
 ):
-    loads = [
-        pltpu.make_async_copy(a, b, sem_in.at[k])
-        for k, (a, b) in enumerate(
-            [(r1.at[pl.ds(core * FF + n * 1024, 1024)], v1.at[pl.ds(core * FF + n * 1024, 1024)])
-             for n in range(2) for core in range(2)]
-            + [(r2, v2), (r3, v3), (out_win, w1), (lon_rims, rims), (lat_blocks, blocks), (gtok_win, w2)]
-        )
+    halves = [
+        [(r1.at[pl.ds(core * FF + n * 1024, 1024)], v1.at[pl.ds(core * FF + n * 1024, 1024)]) for core in range(2)]
+        for n in range(2)
     ]
+    wanted = halves[0] + [(out_win, w1), (lon_rims, rims), (lat_blocks, blocks)] + halves[1]
+    wanted += [(gtok_win, w2), (r2, v2), (r3, v3)]
+    loads = [pltpu.make_async_copy(a, b, sem_in.at[k]) for k, (a, b) in enumerate(wanted)]
     for copy in loads:
         copy.start()
     stores = []
@@ -719,11 +727,7 @@
         copy.start()
         stores.append(copy)
 
-    g_gains[...] = gain_sums[0:2, :]
-    for n in range(8):
-        if n % 4 == 0:
-            loads[n // 2].wait()
-            loads[n // 2 + 1].wait()
+    def wide(n):
         for core in range(2):
             for k in range(2):
                 lanes = slice(k * 256, (k + 1) * 256)
@@ -738,21 +742,8 @@
             cols = pl.ds((n - 1) * 256, 512)
             store(f_up.at[:, cols], g_up.at[:, cols])
             store(f_down.at[cols], g_down.at[cols])
-    loads[4].wait()
-    for part in range(3):
-        for pair in range(4):
-            for core in range(2):
-                f_qkv[core * 256:(core + 1) * 256, part * D + pair * 128:part * D + (pair + 1) * 128] = (
-                    v2[core * 1024 + pair * 256:core * 1024 + (pair + 1) * 256, part * 128:(part + 1) * 128].astype(F32)
-                )
-        cols = pl.ds(part * D, D)
-        store(f_qkv.at[:, cols], g_qkv.at[:, cols])
-    loads[5].wait()
-    f_out[...] = v3[...].astype(F32)
-    store(f_out, g_out)
-    for copy in loads[6:]:
-        copy.wait()
-    for k, (win, out) in enumerate(((w1, outputs), (w2, g_tok))):
+
+    def field(k, win, out):
         for wr in range(2):
             at = (k * 2 + wr) * 2 * PIECE
             src[:HALF, :] = win[wr * HALF:(wr + 1) * HALF, :]
@@ -770,6 +761,33 @@
             inner = blocks[(k * 2 + lev) * BLOCK:(k * 2 + lev + 1) * BLOCK, :].astype(F32)
             full[k, lev * HALF:lev * HALF + BLOCK, :] = (inner + edge).astype(BF16)
         store(full.at[k], out)
+
+    g_gains[...] = gain_sums[0:2, :]
+    for copy in loads[0:2]:
+        copy.wait()
+    for n in range(4):
+        wide(n)
+    for copy in loads[2:5]:
+        copy.wait()
+    field(0, w1, outputs)
+    for copy in loads[5:7]:
+        copy.wait()
+    for n in range(4, 8):
+        wide(n)
+    loads[7].wait()
+    field(1, w2, g_tok)
+    loads[8].wait()
+    for part in range(3):
+        for pair in range(4):
+            for core in range(2):
+                f_qkv[core * 256:(core + 1) * 256, part * D + pair * 128:part * D + (pair + 1) * 128] = (
+                    v2[core * 1024 + pair * 256:core * 1024 + (pair + 1) * 256, part * 128:(part + 1) * 128].astype(F32)
+                )
+        cols = pl.ds(part * D, D)
+        store(f_qkv.at[:, cols], g_qkv.at[:, cols])
+    loads[9].wait()
+    f_out[...] = v3[...].astype(F32)
+    store(f_out, g_out)
     for copy in stores:
         copy.wait()
 

time: 148 us -> 144 us (0.973)
  Pallas kernels: 147 us -> 143 us
    pallas_call x1, Pallas kernels: 135 us -> 133 us  [block(): pl.pallas_call(block_kernel, out_shape=(shape((2 * FF, D), BF16), shape((...]
where the time goes in v4:
time: 144 us
  Pallas kernels  143 us (99%)
    pallas_call x1, Pallas kernels, block(): pl.pallas_call(block_kernel, out_shape=(shape((2 * FF, D), BF16), shape((...  133 us
    pallas_call x1, Pallas kernels, finish_all(): pl.pallas_call(finish_kernel, out_shape=(shape((TOK, D), BF16), shape((TO...  10.2 us

profile of v4, /device:TPU:1, one launch (start us, length us, event | category | flops | bytes accessed | tf_op | source)
XLA Modules:
  0.0 144.0 jit_solution(901556418605184458)
XLA Ops:
  0.6 132.9 %block.1 = (bf16[4096,512]{1,0:T(8,128)(2,1)}, bf16[2048,384]{1,0:T(8,128)(2,1)}, bf16[512,512]{1,0:T(8,128)(2,1)}, f32[8,512]{1,0:T(8,128)}, bf16[1152,512]{1,0...) custom-call(bf16[1152,512]{1,0:T(8,128)(2,1)} %bitcast.4, ...), custom_call_target="tpu_custom_call" | custom-call | tf_op jit(solution)/shard_map/block/pallas_call | solution.py:680
  133.5 10.2 %finish.1 = (bf16[1152,512]{1,0:T(8,128)(2,1)}, bf16[1152,512]{1,0:T(8,128)(2,1)}, f32[512,1536]{1,0:T(8,128)}, f32[512,512]{1,0:T(8,128)}, f32[512,2048]{1,0:T(...) custom-call(bf16[4096,512]{1,0:T(8,128)(2,1)} %get-tuple-element.22.r1, bf16[2048,384]{1,0:T(8,128)(2,1)} %get-tuple-element.23.r2, ...), custom_call_target="tpu_custom_call" | custom-call | tf_op jit(solution)/shard_map/finish/pallas_call | solution.py:800

commit v5 on v4

--- a/solution.py
+++ b/solution.py
@@ -134,7 +134,8 @@
 
 
 class Sums:
-    def __init__(self, own, out, pair, recv1, sum1, recv2, recv3, fin, result, sems, pair_sems):
+    def __init__(self, turn, own, out, pair, recv1, sum1, recv2, recv3, fin, result, sems, pair_sems):
+        self.turn = turn
         self.own, self.out, self.pair = own, out, pair
         self.recv1, self.sum1, self.recv2, self.recv3, self.fin = recv1, sum1, recv2, recv3, fin
         self.result, self.sems, self.pair_sems = result, sems, pair_sems
@@ -143,7 +144,8 @@
         self.base = self.core * own.shape[0]
 
     def flags(self, u, level):
-        turn = lax.rem(u + level, 3) if not isinstance(u, int) else (u + level) % 3
+        turn = u + self.turn + level
+        turn = turn % 3 if isinstance(u, int) else lax.rem(turn, 3)
         first, last = (2 - turn) // 2, turn // 2
         return first, 1 - first - last, last
 
@@ -282,7 +284,7 @@
     refs = iter(rest_refs)
     results = (r1, r2, r3)
     sum_a, sum_b, sum_c = (
-        Sums(*[next(refs) for _ in range(8)], results[k], next(refs), next(refs)) for k in range(3)
+        Sums(TURNS[k], *[next(refs) for _ in range(8)], results[k], next(refs), next(refs)) for k in range(3)
     )
     (rims, send_blocks, gain_slots, gain_part,
      load_sem, halo_s, halo_r, back_s, back_r, gain_s, gain_r) = refs
@@ -447,16 +449,18 @@
     loads[3].wait()
     loads[4].wait()
 
-    def tick(t):
+    def tick(n):
         for stage, lag in reversed(list(zip(sum_a.stages(), LAGS))):
-            u = t - lag
-            if isinstance(t, int):
-                if 0 <= u < 8:
-                    stage(u)
-            else:
-                @pl.when((u >= 0) & (u < 8))
-                def _(stage=stage, u=u):
-                    stage(u)
+            @pl.when(n >= lag)
+            def _(stage=stage, lag=lag):
+                stage(n - lag)
+
+    plan, tail = schedule()
+    all_sums = (sum_a, sum_b, sum_c)
+
+    def due(spot):
+        for which, stage, u in plan.get(spot, ()):
+            all_sums[which].stages()[stage](u)
 
     def share(left, right, flip, own, out, at):
         rows = pl.ds(pl.multiple_of(at, 128), 128)
@@ -489,7 +493,7 @@
         tick(n)
 
     loop(0, FF // wide, columns)
-    tick(8)
+    due(8)
     gain_part[...] = jnp.zeros_like(gain_part)
 
     def finish(rows):
@@ -504,7 +508,9 @@
         hid[rows, :] = g
         g_ctx[rows, :] = mm_nt(g, w_out[...]).astype(BF16)
 
-    rows_loop(TOK, WIN, finish)
+    rows_loop(TOK // 2, WIN, finish)
+    due(8.5)
+    rows_loop(TOK // 2, WIN, lambda rows: finish(pl.ds(pl.multiple_of(rows.start + TOK // 2, WIN), WIN)))
     backs = []
 
     def send_back(k, win):
@@ -527,14 +533,14 @@
     send_back(0, out_win)
     gmix, g_att = acc_in, hid
 
-    tick(9)
+    due(9)
     hid_t[...] = lowered[...].T
     c_t[...] = context[...].T
     for which, dst in ((core, sum_c.own), (1 - core, sum_c.out)):
         part = mm(c_t[pl.ds(pl.multiple_of(which * 256, 256), 256), :], g_att[...])
         dst[...] = part.astype(dst.dtype)
     sum_c.hand(0).start()
-    tick(10)
+    due(10)
 
     def attend_back(w, pair):
         rows = pl.ds(pl.multiple_of(w * WIN, WIN), WIN)
@@ -560,19 +566,15 @@
         for at, value in zip(lanes, sums):
             g_pack[rows, at] = value.astype(BF16)
 
-    both = (sum_b, sum_c)
-
     def heads(pair):
         def some(k):
             for w in range(4):
                 attend_back(k * 4 + w, pair)
-            now = 2 * pair + k
-            for when, which, stage, u in LATE:
-                @pl.when(now == when)
-                def _(which=which, stage=stage, u=u):
-                    both[which].stages()[stage](u)
-
-            tick(11 + now)
+            for spot in range(11, 19):
+                if spot in plan:
+                    @pl.when(2 * pair + k == spot - 11)
+                    def _(spot=spot):
+                        due(spot)
 
         loop(0, 2, some)
         cols = pl.ds(pl.multiple_of(pair * 384, 384), 384)
@@ -584,7 +586,7 @@
                 sum_b.hand(pair).start()
 
     loop(0, 4, heads)
-    tick(19)
+    due(19)
 
     def finish_back(rows):
         g_low = mm_nt(g_pack[rows, :], w_qkv[...]).astype(BF16).astype(F32)
@@ -592,20 +594,15 @@
         gain_part[0:1, :] += jnp.sum(g_low * normed, 0, keepdims=True)
         gtok_win[rows, :] = (gmix[rows, :] + norm_back(g_low, normed, inv_std, gain_a)).astype(BF16)
 
-    def later(phase):
-        for which, stage, u in PHASES[phase]:
-            both[which].stages()[stage](u)
-
     rows_loop(TOK // 2, 288, finish_back)
-    later(0)
-    tick(20)
+    due(20)
     rows_loop(TOK // 2, 288, lambda rows: finish_back(pl.ds(pl.multiple_of(rows.start + TOK // 2, 288), 288)))
     send_back(1, gtok_win)
-    later(1)
-    tick(21)
     gain_slots[0, 0] = gain_part[...]
     gain_pair = remote(gain_slots.at[0, 0], gain_slots.at[0, 1], gain_s.at[0, 0], gain_r.at[0, 0], partner)
     gain_pair.start()
+    due(21)
+
     def gains_along(level, total):
         axis = level - 1
         slot = gain_slots.at[level, place[axis]]
@@ -623,17 +620,17 @@
             copy.wait()
         return (gain_slots[level, 0] + gain_slots[level, 1]) + (gain_slots[level, 2] + gain_slots[level, 3])
 
-    gain_pair.wait()
-    gain_copies = gains_along(1, gain_slots[0, 0] + gain_slots[0, 1])
-    later(2)
-    tick(22)
-    gain_copies = gains_along(2, gains_sum(1, gain_copies))
-    later(3)
-    tick(23)
-    gain_copies = gains_along(3, gains_sum(2, gain_copies))
-    later(4)
-    gains_out[...] = gains_sum(3, gain_copies) * SCALE
-    later(5)
+    gain_copies = []
+    for which, stage, u in tail:
+        if which < 3:
+            all_sums[which].stages()[stage](u)
+        elif stage == 0:
+            gain_pair.wait()
+            gain_copies = gains_along(1, gain_slots[0, 0] + gain_slots[0, 1])
+        elif stage < 3:
+            gain_copies = gains_along(stage + 1, gains_sum(stage, gain_copies))
+        else:
+            gains_out[...] = gains_sum(3, gain_copies) * SCALE
     loop(0, 8, sum_a.end)
     sum_c.end(0)
     loop(0, 4, sum_b.end)
@@ -641,19 +638,33 @@
         copy.wait()
 
 
-LAGS = (1, 4, 7, 10, 13, 16)
-LATE = (
-    (0, 1, 0, 0), (2, 1, 1, 0), (4, 1, 2, 0), (6, 1, 3, 0),
-    (6, 0, 2, 0), (4, 0, 1, 0), (2, 0, 0, 0), (6, 0, 1, 1), (4, 0, 0, 1), (6, 0, 0, 2),
-)
-PHASES = (
-    ((1, 4, 0), (0, 3, 0), (0, 2, 1), (0, 1, 2), (0, 0, 3)),
-    ((1, 5, 0), (0, 4, 0), (0, 3, 1), (0, 2, 2), (0, 1, 3)),
-    ((0, 5, 0), (0, 4, 1), (0, 3, 2), (0, 2, 3)),
-    ((0, 5, 1), (0, 4, 2), (0, 3, 3)),
-    ((0, 5, 2), (0, 4, 3)),
-    ((0, 5, 3),),
-)
+LAGS = (1, 5, 8, 11, 14, 17)
+BLOCK_US = 2.9
+TURNS = (0, 2, 0)
+SPOTS = dict(enumerate((23.2, 29.2, 32.2, 34.0, 35.7, 38.6, 40.3, 43.2, 44.9, 47.8, 49.5, 50.6, 52.8, 56.0), 8))
+SPOTS[8.5] = 26.2
+PAIRS_US = (36.8, 41.4, 46.0, 50.6)
+STAGES_US = (2.0, 10.0, 8.0, 8.0, 7.0, 10.0)
+
+
+def schedule():
+    units = [(0, u, BLOCK_US * (u + 1)) for u in range(8)]
+    units += [(2, 0, SPOTS[10])] + [(1, u, PAIRS_US[u]) for u in range(4)]
+    plan, tail = {}, []
+    for which, u, at in units:
+        for stage, length in enumerate(STAGES_US):
+            if which == 0 and u + LAGS[stage] < 8:
+                at = BLOCK_US * (u + LAGS[stage] + 1)
+                continue
+            at = at + length
+            spots = [k for k in sorted(SPOTS) if SPOTS[k] >= at - 0.3]
+            if spots:
+                plan.setdefault(spots[0], []).append((at, which, stage, u))
+                at = max(at, SPOTS[spots[0]])
+            else:
+                tail.append((at, which, stage, u))
+    tail += [(SPOTS[21] + 2.0 + 5.5 * stage, 3, stage, 0) for stage in range(4)]
+    return {k: [e[1:] for e in sorted(v)] for k, v in plan.items()}, [e[1:] for e in sorted(tail)]
 
 
 def sums_scratch(units, lanes):

time: 144 us -> 136 us (0.944)
  Pallas kernels: 143 us -> 135 us
    pallas_call x1, Pallas kernels: 133 us -> 125 us  [block(): pl.pallas_call(block_kernel, out_shape=(shape((2 * FF, D), BF16), shape((...]
where the time goes in v5:
time: 136 us
  Pallas kernels  135 us (99%)
    pallas_call x1, Pallas kernels, block(): pl.pallas_call(block_kernel, out_shape=(shape((2 * FF, D), BF16), shape((...  125 us
    pallas_call x1, Pallas kernels, finish_all(): pl.pallas_call(finish_kernel, out_shape=(shape((TOK, D), BF16), shape((TO...  10.2 us

profile of v5, /device:TPU:1, one launch (start us, length us, event | category | flops | bytes accessed | tf_op | source)
XLA Modules:
  0.0 136.1 jit_solution(13704538605877796758)
XLA Ops:
  0.6 125.1 %block.1 = (bf16[4096,512]{1,0:T(8,128)(2,1)}, bf16[2048,384]{1,0:T(8,128)(2,1)}, bf16[512,512]{1,0:T(8,128)(2,1)}, f32[8,512]{1,0:T(8,128)}, bf16[1152,512]{1,0...) custom-call(bf16[1152,512]{1,0:T(8,128)(2,1)} %bitcast.4, ...), custom_call_target="tpu_custom_call" | custom-call | tf_op jit(solution)/shard_map/block/pallas_call | solution.py:691
  125.7 10.2 %finish.1 = (bf16[1152,512]{1,0:T(8,128)(2,1)}, bf16[1152,512]{1,0:T(8,128)(2,1)}, f32[512,1536]{1,0:T(8,128)}, f32[512,512]{1,0:T(8,128)}, f32[512,2048]{1,0:T(...) custom-call(bf16[4096,512]{1,0:T(8,128)(2,1)} %get-tuple-element.22.r1, bf16[2048,384]{1,0:T(8,128)(2,1)} %get-tuple-element.23.r2, ...), custom_call_target="tpu_custom_call" | custom-call | tf_op jit(solution)/shard_map/finish/pallas_call | solution.py:811

commit v6 on v5

--- a/solution.py
+++ b/solution.py
@@ -391,12 +391,8 @@
     def first_part(first, last):
         band = slice(first * WIN, last * WIN)
 
-        def first_norm(i):
-            rows = pl.ds(pl.multiple_of(i * WIN, WIN), WIN)
-            normed, _ = norm_stats(x_ref[rows, :].astype(F32))
-            lowered[rows, :] = (normed * gain_a).astype(BF16)
-
-        loop(first, last, first_norm)
+        normed, _ = norm_stats(x_ref[band, :].astype(F32))
+        lowered[band, :] = (normed * gain_a).astype(BF16)
 
         def project(n):
             cols = pl.ds(pl.multiple_of(n * 256, 256), 256)
@@ -441,7 +437,7 @@
         normed, _ = norm_stats(m)
         hid[rows, :] = (normed * gain_b).astype(BF16)
 
-    rows_loop(TOK, 288, second_norm)
+    rows_loop(TOK, 576, second_norm)
     hid_t[...] = hid[...].T
     c_t[...] = c_ref[...].T
     acc_out[...] = jnp.zeros_like(acc_out)
@@ -508,9 +504,9 @@
         hid[rows, :] = g
         g_ctx[rows, :] = mm_nt(g, w_out[...]).astype(BF16)
 
-    rows_loop(TOK // 2, WIN, finish)
+    rows_loop(TOK // 2, 576, finish)
     due(8.5)
-    rows_loop(TOK // 2, WIN, lambda rows: finish(pl.ds(pl.multiple_of(rows.start + TOK // 2, WIN), WIN)))
+    rows_loop(TOK // 2, 576, lambda rows: finish(pl.ds(pl.multiple_of(rows.start + TOK // 2, 576), 576)))
     backs = []
 
     def send_back(k, win):
@@ -594,9 +590,9 @@
         gain_part[0:1, :] += jnp.sum(g_low * normed, 0, keepdims=True)
         gtok_win[rows, :] = (gmix[rows, :] + norm_back(g_low, normed, inv_std, gain_a)).astype(BF16)
 
-    rows_loop(TOK // 2, 288, finish_back)
+    rows_loop(TOK // 2, 576, finish_back)
     due(20)
-    rows_loop(TOK // 2, 288, lambda rows: finish_back(pl.ds(pl.multiple_of(rows.start + TOK // 2, 288), 288)))
+    rows_loop(TOK // 2, 576, lambda rows: finish_back(pl.ds(pl.multiple_of(rows.start + TOK // 2, 576), 576)))
     send_back(1, gtok_win)
     gain_slots[0, 0] = gain_part[...]
     gain_pair = remote(gain_slots.at[0, 0], gain_slots.at[0, 1], gain_s.at[0, 0], gain_r.at[0, 0], partner)
@@ -641,9 +637,9 @@
 LAGS = (1, 5, 8, 11, 14, 17)
 BLOCK_US = 2.9
 TURNS = (0, 2, 0)
-SPOTS = dict(enumerate((23.2, 29.2, 32.2, 34.0, 35.7, 38.6, 40.3, 43.2, 44.9, 47.8, 49.5, 50.6, 52.8, 56.0), 8))
-SPOTS[8.5] = 26.2
-PAIRS_US = (36.8, 41.4, 46.0, 50.6)
+SPOTS = dict(enumerate((23.2, 27.2, 30.2, 32.0, 33.7, 36.6, 38.3, 41.2, 42.9, 45.8, 47.5, 48.6, 50.6, 53.5), 8))
+SPOTS[8.5] = 25.0
+PAIRS_US = (34.8, 39.4, 44.0, 48.6)
 STAGES_US = (2.0, 10.0, 8.0, 8.0, 7.0, 10.0)
 
 

time: 136 us -> 134 us (0.985)
  Pallas kernels: 135 us -> 133 us
    pallas_call x1, Pallas kernels: 125 us -> 122 us  [block(): pl.pallas_call(block_kernel, out_shape=(shape((2 * FF, D), BF16), shape((...]
where the time goes in v6:
time: 134 us
  Pallas kernels  133 us (99%)
    pallas_call x1, Pallas kernels, block(): pl.pallas_call(block_kernel, out_shape=(shape((2 * FF, D), BF16), shape((...  122 us
    pallas_call x1, Pallas kernels, finish_all(): pl.pallas_call(finish_kernel, out_shape=(shape((TOK, D), BF16), shape((TO...  10.2 us

profile of v6, /device:TPU:1, one launch (start us, length us, event | category | flops | bytes accessed | tf_op | source)
XLA Modules:
  0.0 133.5 jit_solution(6276047547453142503)
XLA Ops:
  0.6 122.5 %block.1 = (bf16[4096,512]{1,0:T(8,128)(2,1)}, bf16[2048,384]{1,0:T(8,128)(2,1)}, bf16[512,512]{1,0:T(8,128)(2,1)}, f32[8,512]{1,0:T(8,128)}, bf16[1152,512]{1,0...) custom-call(bf16[1152,512]{1,0:T(8,128)(2,1)} %bitcast.4, ...), custom_call_target="tpu_custom_call" | custom-call | tf_op jit(solution)/shard_map/block/pallas_call | solution.py:687
  123.1 10.2 %finish.1 = (bf16[1152,512]{1,0:T(8,128)(2,1)}, bf16[1152,512]{1,0:T(8,128)(2,1)}, f32[512,1536]{1,0:T(8,128)}, f32[512,512]{1,0:T(8,128)}, f32[512,2048]{1,0:T(...) custom-call(bf16[4096,512]{1,0:T(8,128)(2,1)} %get-tuple-element.22.r1, bf16[2048,384]{1,0:T(8,128)(2,1)} %get-tuple-element.23.r2, ...), custom_call_target="tpu_custom_call" | custom-call | tf_op jit(solution)/shard_map/finish/pallas_call | solution.py:807
